TPU v7x, 32 devices: a whole 2x2x4 slice. The times are simulated.
32 devices in a mesh: grp: 2 (over y), view: 4 (over z), slab: 2 (over x), rep: 2 (over core).
Axes of the slice: x: 2, y: 2, z: 4, core: 2. Of those that a mesh axis runs over, the one named last changes fastest.
Arguments:
- images: float32 [3, 4, 512, 512], P(None, ('grp', 'slab'), ('view', 'rep')), parts along dimension 1, may hold values from -6 to 6
- scaled_duals: float32 [9, 4, 512, 512], P(None, ('grp', 'slab'), ('view', 'rep')), parts along dimension 1, may hold values from -3 to 3
- proj_tiles: bfloat16 [48, 128, 128], replicated, may hold values from -0.5 to 0.5
- tile_ids: int32 [4, 256], replicated, may hold values from 0 to 47
- pixel_blocks: int32 [4, 256], replicated, may hold values from 0 to 2047
- tof_offsets: int32 [4, 256], replicated, may hold values from 0 to 1920
- counts: int32 [4], replicated, may hold values from 32 to 256, as said below
- sinogram: bfloat16 [4, 8192], P(('grp', 'slab')), parts along dimension 0, may hold values from -12 to 12
- coil_maps: float32 [2, 4, 4, 4, 2, 64, 512], P(None, 'view', ('grp', 'slab'), None, 'rep'), parts along dimension 2, may hold values from -2.1213202 to 2.1213202
- kspace: float32 [2, 4, 4, 4, 2, 64, 512], P(None, 'view', ('grp', 'slab'), None, 'rep'), parts along dimension 2, may hold values from -0.9 to 0.9
- sampling: int32 [4, 4, 2, 64], P(('grp', 'slab'), None, 'rep'), parts along dimension 0, may hold values 0 or 1
Outputs:
- updated: float32 [3, 4, 512, 512], P(None, ('grp', 'slab'), ('view', 'rep')), parts along dimension 1
- shrunk: float32 [9, 4, 512, 512], P(None, ('grp', 'slab'), ('view', 'rep')), parts along dimension 1
- dual_next: float32 [9, 4, 512, 512], P(None, ('grp', 'slab'), ('view', 'rep')), parts along dimension 1
There are 2 independent parts, one for each index of `grp`. A program takes and returns all parts, laid end to end along the dimension named above; an argument that names none is the same for every part. Nothing has to cross between parts.
Inputs may be any that keep to these rules, and one draw needn't show every extreme that they name: Slots j < counts[v] of sector v are live and the others unused; some sector has all 256 slots live.
All inputs are finite; a program needn't handle non-finite values. No bound on the sum of `sampling` on one device may be relied on, other than what follows from the above.
Results may differ from a plain program's by a relative error of at most 0.0024.
Values sent between devices are 32-bit elements; how exact they have to be, the bound alone decides.
A program may use at most 64 MiB of HBM per device.

v0:
```python
import math

import jax
import jax.numpy as jnp
from jax import lax
from jax.sharding import PartitionSpec as P

kappa = 4.0
step_size = 0.4
penalty = 0.5
highest = lax.Precision.HIGHEST


def padded(cells, sides, width):
    for axis, dim in sides:
        count = lax.axis_size(axis)
        ends = count - 1
        head = lax.slice_in_dim(cells, 0, width, axis=dim)
        tail = lax.slice_in_dim(cells, cells.shape[dim] - width, cells.shape[dim], axis=dim)
        cells = jnp.concatenate(
            [
                lax.ppermute(tail, axis, [(i, (i + 1) % count) for i in range(ends)]),
                cells,
                lax.ppermute(head, axis, [((i + 1) % count, i) for i in range(ends)]),
            ],
            axis=dim,
        )
    return cells


def matmul(left, right):
    return jnp.dot(left, right, precision=highest, preferred_element_type=jnp.float32)


def dft_table(row_index, length):
    column_index = jnp.arange(length, dtype=jnp.int32)
    phase = row_index[:, None] * column_index[None, :] % length
    angle = phase.astype(jnp.float32) * (2.0 * math.pi / length)
    factor = 1.0 / math.sqrt(length)
    return (jnp.cos(angle) * factor, jnp.sin(angle) * factor)


def pair_rows(values, groups, row_block):
    length = values.shape[-1]
    pieces = values.reshape(2, groups, 1, row_block, length)
    joined = lax.all_gather(pieces, "rep", axis=2, tiled=True)
    return joined.reshape(2, -1, length)


def on_device(
    images,
    scaled_duals,
    proj_tiles,
    tile_ids,
    pixel_blocks,
    tof_offsets,
    counts,
    sinogram,
    coil_maps,
    kspace,
    sampling,
):
    rep_count = lax.axis_size("rep")
    view_at = lax.axis_index("view")
    rep_at = lax.axis_index("rep")
    owner_at = view_at * rep_count + rep_at
    row_block = images.shape[2]
    width = images.shape[3]
    tile_size = proj_tiles.shape[1]
    sectors = counts.shape[0]
    capacity = tile_ids.shape[1]
    sector_bins = sinogram.shape[1] // sectors
    group = 16
    lane_index = jnp.arange(tile_size, dtype=jnp.int32)
    gathered = lax.all_gather(images, ("view", "rep"), axis=2, tiled=True)
    pixel_rows = gathered[0, 0].astype(jnp.bfloat16).reshape(-1, tile_size)
    flat_ids = tile_ids.reshape(-1)
    flat_blocks = pixel_blocks.reshape(-1)
    flat_offsets = tof_offsets.reshape(-1)
    own_count = lax.dynamic_index_in_dim(counts, view_at, keepdims=False)
    item_count = jnp.maximum(own_count - rep_at + rep_count - 1, 0) // rep_count

    def lookup(item):
        slot = rep_at + rep_count * item
        sector = view_at + jnp.zeros_like(item)
        return (sector, slot, jnp.zeros_like(item), slot < own_count)

    def fetch(block_step):
        item = block_step * group + jnp.arange(group, dtype=jnp.int32)
        sector, slot, offset_base, live_flag = lookup(item)
        flat = sector * capacity + jnp.clip(slot, 0, capacity - 1)
        tile_mats = proj_tiles[flat_ids[flat]]
        block_index = flat_blocks[flat]
        positions = flat_offsets[flat][:, None] + lane_index[None, :]
        return (tile_mats, block_index, positions, live_flag.astype(jnp.float32)[:, None])

    block_count = (item_count + group - 1) // group

    def forward_block(block_step, sino_part):
        tile_mats, block_index, positions, live_flag = fetch(block_step)
        contrib = jnp.einsum(
            "gbt,gt->gb", tile_mats, pixel_rows[block_index], preferred_element_type=jnp.float32
        )
        return sino_part.at[positions].add(contrib * live_flag)

    projected = lax.fori_loop(0, block_count, forward_block, jnp.zeros((sector_bins,), jnp.float32))
    full_sino = lax.psum(projected, "rep")
    measured = lax.dynamic_slice_in_dim(sinogram[0], view_at * sector_bins, sector_bins).astype(
        jnp.float32
    )
    pet_residual = (full_sino - measured).astype(jnp.bfloat16)

    def back_block(block_step, partial_value):
        tile_mats, block_index, positions, live_flag = fetch(block_step)
        back = jnp.einsum(
            "gbt,gb->gt", tile_mats, pet_residual[positions], preferred_element_type=jnp.float32
        )
        return partial_value.at[block_index].add(back * live_flag)

    back_projected = lax.fori_loop(
        0, block_count, back_block, jnp.zeros((width * width // tile_size, tile_size), jnp.float32)
    )
    groups = coil_maps.shape[3]
    local_rows = (
        (jnp.arange(groups, dtype=jnp.int32)[:, None] * rep_count + rep_at) * row_block
        + jnp.arange(row_block, dtype=jnp.int32)[None, :]
    ).reshape(-1)
    cos_full, sin_full = dft_table(jnp.arange(width, dtype=jnp.int32), width)
    cos_part, sin_part = dft_table(local_rows, width)
    own_image = lax.dynamic_index_in_dim(
        gathered[1:3, 0].reshape(2, groups, rep_count, row_block, width), rep_at, 2, keepdims=False
    ).reshape(2, groups * row_block, width)
    sens = coil_maps.reshape(2, groups * row_block, width)
    coil_re = sens[0] * own_image[0] - sens[1] * own_image[1]
    coil_im = sens[0] * own_image[1] + sens[1] * own_image[0]
    column_re = matmul(coil_re, cos_full) + matmul(coil_im, sin_full)
    column_im = matmul(coil_im, cos_full) - matmul(coil_re, sin_full)
    column_all = pair_rows(jnp.stack([column_re, column_im]), groups, row_block)
    spec_re = matmul(cos_part, column_all[0]) + matmul(sin_part, column_all[1])
    spec_im = matmul(cos_part, column_all[1]) - matmul(sin_part, column_all[0])
    measured_k = kspace.reshape(2, groups * row_block, width)
    acquired_samples = sampling.reshape(-1).astype(jnp.float32)[:, None]
    resid_re = acquired_samples * (spec_re - measured_k[0])
    resid_im = acquired_samples * (spec_im - measured_k[1])
    inverse_re = matmul(resid_re, cos_full) - matmul(resid_im, sin_full)
    inverse_im = matmul(resid_im, cos_full) + matmul(resid_re, sin_full)
    inverse_all = pair_rows(jnp.stack([inverse_re, inverse_im]), groups, row_block)
    image_re = matmul(cos_part, inverse_all[0]) - matmul(sin_part, inverse_all[1])
    image_im = matmul(cos_part, inverse_all[1]) + matmul(sin_part, inverse_all[0])
    grad_re = sens[0] * image_re + sens[1] * image_im
    grad_im = sens[0] * image_im - sens[1] * image_re
    pet_term = back_projected.reshape(1, groups, rep_count, row_block, width)
    coil_rows = jnp.stack([grad_re, grad_im]).reshape(2, groups, 1, row_block, width)
    picked = (jnp.arange(rep_count) == rep_at).astype(jnp.float32)[None, None, :, None, None]
    term = jnp.concatenate([pet_term, coil_rows * picked], axis=0).reshape(
        3, 1, groups * rep_count, row_block, width
    )
    data_gradient = lax.psum_scatter(
        term, ("view", "rep"), scatter_dimension=2, tiled=True
    ).reshape(3, 1, row_block, width)
    stacked = jnp.concatenate([images, scaled_duals], axis=0)
    extended = padded(stacked, ((("view", "rep"), 2), ("slab", 1)), 1)
    slab_count = lax.axis_size("slab")
    slab_at = lax.axis_index("slab")
    global_rows = owner_at * row_block - 1 + jnp.arange(row_block + 1, dtype=jnp.int32)
    global_slices = slab_at - 1 + jnp.arange(2, dtype=jnp.int32)
    inside = ((global_rows >= 0)[None, :, None] & (global_slices >= 0)[:, None, None]).astype(
        jnp.float32
    )
    row_keep = (global_rows < width - 1).astype(jnp.float32)[None, :, None]
    slice_keep = (global_slices < slab_count - 1).astype(jnp.float32)[:, None, None]
    column_keep = (jnp.arange(width) < width - 1).astype(jnp.float32)[None, None, :]
    source = extended[:3]
    region = source[:, 0:2, 0 : row_block + 1]
    diff_rows = (source[:, 0:2, 1 : row_block + 2] - region) * row_keep * inside
    next_column = jnp.concatenate([region[..., 1:], jnp.zeros_like(region[..., :1])], axis=-1)
    diff_columns = (next_column - region) * column_keep * inside
    diff_slices = (source[:, 1:3, 0 : row_block + 1] - region) * slice_keep * inside
    differences = jnp.stack([diff_rows, diff_columns, diff_slices], axis=1).reshape(
        9, 2, row_block + 1, width
    )
    spread = differences + extended[3:, 0:2, 0 : row_block + 1]
    magnitude = jnp.sqrt(jnp.sum(spread * spread, axis=0))
    shrunk = spread * (jnp.maximum(magnitude - kappa, 0.0) / jnp.maximum(magnitude, kappa))[None]
    dual_next = spread - shrunk
    coupling = (differences - shrunk + dual_next).reshape(3, 3, 2, row_block + 1, width)
    couple_rows = coupling[:, 0] * row_keep
    couple_columns = coupling[:, 1] * column_keep
    couple_slices = coupling[:, 2] * slice_keep
    adjoint_rows = couple_rows[:, 1, 0:row_block] - couple_rows[:, 1, 1 : row_block + 1]
    own_columns = couple_columns[:, 1, 1 : row_block + 1]
    adjoint_columns = (
        jnp.concatenate([jnp.zeros_like(own_columns[..., :1]), own_columns[..., :-1]], axis=-1)
        - own_columns
    )
    adjoint_slices = couple_slices[:, 0, 1 : row_block + 1] - couple_slices[:, 1, 1 : row_block + 1]
    adjoint = (adjoint_rows + adjoint_columns + adjoint_slices)[:, None]
    updated = images - step_size * (data_gradient + penalty * adjoint)
    return (updated, shrunk[:, 1:2, 1 : row_block + 1], dual_next[:, 1:2, 1 : row_block + 1])


def solution(mesh):
    placed = (
        P(None, ("grp", "slab"), ("view", "rep"), None),
        P(None, ("grp", "slab"), ("view", "rep"), None),
        P(),
        P(),
        P(),
        P(),
        P(),
        P(("grp", "slab"), None),
        P(None, "view", ("grp", "slab"), None, "rep", None, None),
        P(None, "view", ("grp", "slab"), None, "rep", None, None),
        P(("grp", "slab"), None, "rep", None),
    )
    return jax.shard_map(
        on_device,
        mesh=mesh,
        in_specs=placed,
        out_specs=(
            P(None, ("grp", "slab"), ("view", "rep"), None),
            P(None, ("grp", "slab"), ("view", "rep"), None),
            P(None, ("grp", "slab"), ("view", "rep"), None),
        ),
        check_vma=False,
    )
```

profile of v0, /device:TPU:10, one launch (start us, length us, event | category | flops | bytes accessed | tf_op | source)
XLA Modules:
  0.0 536.3 jit_solution(4841216148539440434)
XLA Ops:
  8.0 1.3 dynamic_slice.11
  10.1 0.7 convert_reduce_fusion
  10.9 0.7 copy.122
  12.3 0.7 copy.123
  13.0 0.7 dynamic-slice_convert_fusion
  13.7 1.3 fusion.191
  15.0 1.0 fusion.190
  16.0 32.1 %all-gather.4.cloned.1.call-done = f32[3,1,512,512]{3,2,1,0:T(8,128)} async-done(((f32[3,1,64,512]{3,2,1,0:T(8,128)}), f32[3,1,512,512]{3,2,1,0:T(8,128)}) %all-gather.4.cloned.1.call-update) | async-done | bytes 3145744 | tf_op jit(solution)/shard_map/all_gather | solution.py:75
  48.1 1.3 slice.216
  49.7 1.6 slice-done
  51.7 5.3 fusion.46
  57.1 5.3 fusion.45
  62.4 5.4 %convolution_add_fusion.3 = f32[256,512]{1,0:T(8,128)S(1)} fusion(f32[256,512]{1,0:T(8,128)S(1)} %fusion.46, f32[256,512]{1,0:T(8,128)S(1)} %get-tuple-element.410), kind=kOutput, calls=%fused_computation.67 | convolution fusion | flops 809369600 | bytes 1572864 | tf_op jit(solution)/shard_map/dot_general | solution.py:32
  67.8 5.4 convolution_subtract_fusion.3
  73.2 1.0 pad_maximum_fusion.4
  74.9 38.3 %while.26 = (s32[]{:T(128)}, f32[2048]{0:T(1024)S(1)}, s32[]{:T(128)}, s32[]{:T(128)}, s32[]{:T(128)}, /*index=5*/s32[1024]{0:T(1024)S(1)}, s32[1024]{0:T(1024)S...) while((s32[]{:T(128)}, f32[2048]{0:T(1024)S(1)}, ...), condition=%wide.region_2.3_spmd.clone, body=%wide.region_0.2_spmd.clone.sunk | while | flops 539955 | bytes 5858905 | solution.py:106
  79.4 14.7 %scatter_fusion = f32[2048]{0:T(1024)S(1)} fusion(f32[2048]{0:T(1024)S(1)} %get-tuple-element.573, s32[2048]{0:T(1024)S(1)} %fusion.228, f32[2048]{0:T(1024)S(1)} %multiply_bitcast_fusion.2), kind=kCustom, calls=%fused_computation.10.clone.clone.1 | custom fusion | flops 2048 | bytes 32768 | tf_op jit(solution)/shard_map/while/body/scatter-add | solution.py:104
  98.5 14.7 %scatter_fusion = f32[2048]{0:T(1024)S(1)} fusion(f32[2048]{0:T(1024)S(1)} %get-tuple-element.573, s32[2048]{0:T(1024)S(1)} %fusion.228, f32[2048]{0:T(1024)S(1)} %multiply_bitcast_fusion.2), kind=kCustom, calls=%fused_computation.10.clone.clone.1 | custom fusion | flops 2048 | bytes 32768 | tf_op jit(solution)/shard_map/while/body/scatter-add | solution.py:104
  113.2 2.5 psum.7
  115.7 1.8 fusion.189
  117.5 3.1 fusion.84
  120.6 3.1 fusion.85
  123.7 3.1 fusion.24
  126.8 16.0 %fusion.43 = f32[256,512]{1,0:T(8,128)S(1)} fusion(f32[256,512]{1,0:T(8,128)S(1)} %fusion.24), kind=kOutput, calls=%fused_computation.112 | convolution fusion | flops 809238528 | bytes 1048576 | tf_op jit(solution)/shard_map/dot_general | solution.py:32
  142.8 3.1 fusion.25
  145.9 5.3 fusion.44
  151.2 5.4 %convolution_add_fusion.1 = f32[256,512]{1,0:T(8,128)S(1)} fusion(f32[256,512]{1,0:T(8,128)S(1)} %fusion.43, f32[256,512]{1,0:T(8,128)S(1)} %fusion.25), kind=kOutput, calls=%fused_computation.62 | convolution fusion | flops 809369600 | bytes 1572864 | tf_op jit(solution)/shard_map/dot_general | solution.py:32
  156.6 5.4 convolution_subtract_fusion.1
  162.0 1.0 pad_maximum_fusion.5
  163.1 1.0 broadcast_in_dim.4
  164.1 39.5 %while.27 = (s32[]{:T(128)}, f32[2048,128]{1,0:T(8,128)}, s32[]{:T(128)}, s32[]{:T(128)}, s32[]{:T(128)}, /*index=5*/s32[1024]{0:T(1024)S(1)}, s32[1024]{0:T(102...) while((s32[]{:T(128)}, f32[2048,128]{1,0:T(8,128)}, ...), condition=%wide.region_6.7_spmd.clone, body=%wide.region_4.6_spmd.clone.sunk | while | flops 540979 | bytes 2676577 | solution.py:120
  166.8 13.1 %gather_fusion.9 = bf16[2048]{0:T(1024)(128)(2,1)S(1)} fusion(bf16[2048]{0:T(1024)(128)(2,1)S(1)} %get-tuple-element.633, s32[2048]{0:T(1024)S(1)} %fusion.238), kind=kCustom, calls=%fused_computation.9.clone.clone.1 | custom fusion | bytes 16384 | tf_op jit(solution)/shard_map/while/body/gather | solution.py:116
  180.8 2.9 scatter_custom_fusion.10
  186.4 13.1 %gather_fusion.9 = bf16[2048]{0:T(1024)(128)(2,1)S(1)} fusion(bf16[2048]{0:T(1024)(128)(2,1)S(1)} %get-tuple-element.633, s32[2048]{0:T(1024)S(1)} %fusion.238), kind=kCustom, calls=%fused_computation.9.clone.clone.1 | custom fusion | bytes 16384 | tf_op jit(solution)/shard_map/while/body/gather | solution.py:116
  200.4 2.9 scatter_custom_fusion.10
  203.6 1.4 concatenate.30
  205.1 83.6 %all-gather.8.cloned.1.call-done = f32[2,4,2,64,512]{4,3,2,1,0:T(8,128)} async-done(((f32[2,4,1,64,512]{4,3,2,1,0:T(8,128)}), f32[2,4,2,64,512]{4,3,2,1,0:T(8,128)}) %all-gather.8.cloned.1.call-update) | async-done | bytes 2097168 | tf_op jit(solution)/shard_map/all_gather | solution.py:46
  288.7 1.8 fusion.188
  290.5 3.1 fusion.83
  293.5 3.1 fusion.82
  296.6 3.1 convolution_subtract_fusion
  299.7 3.4 fusion.52
  303.9 2.1 pad_maximum_fusion
  306.0 1.2 copy-done.1
  307.4 2.2 collective-permute-start
  309.6 35.5 %collective-permute-start.1 = (f32[12,1,1,512]{3,2,0,1:T(1,128)S(1)}, f32[12,1,1,512]{3,2,0,1:T(1,128)S(1)}, u32[]{:S(2)}, u32[]{:S(2)}) collective-permute-start(f32[12,1,1,512]{3,2,0,1:T(1,128)S(1)} %get-tuple-element.414), channel_id=1, source_target_pairs={{1,0},{4,1},{5,4},{8,5},{9,8},{12,9},{13,12},{3,2},{6,3},{7,6},{10... | collective-permute-start | bytes 73736 | tf_op jit(solution)/shard_map/ppermute | solution.py:24
  345.1 116.8 %collective-permute-done.1 = f32[12,1,1,512]{3,2,0,1:T(1,128)S(1)} collective-permute-done((f32[12,1,1,512]{3,2,0,1:T(1,128)S(1)}, f32[12,1,1,512]{3,2,0,1:T(1,128)S(1)}, u32[]{:S(2)}, u32[]{:S(2)}) %collective-permute-start.1) | collective-permute-done | bytes 24608 | tf_op jit(solution)/shard_map/ppermute | solution.py:24
  462.2 1.7 copy.89
  463.9 3.7 collective-permute-start.3
  467.6 1.3 collective-permute-start.2
  469.1 30.3 %collective-permute-done.3 = f32[12,1,66,512]{3,1,2,0:T(1,128)} collective-permute-done((f32[12,1,66,512]{3,1,2,0:T(1,128)S(1)}, f32[12,1,66,512]{3,1,2,0:T(1,128)}, u32[]{:S(2)}, u32[]{:S(2)}) %collective-permute-start.3) | collective-permute-done | bytes 1622048 | tf_op jit(solution)/shard_map/ppermute | solution.py:24
  499.5 1.6 copy.98
  501.1 4.4 collective-permute-done.2
  505.4 3.9 pad_maximum_fusion.11
  509.8 1.4 fusion.41
  511.3 1.2 pad_maximum_fusion.2
  512.4 0.8 copy.100
  513.3 4.3 multiply_reduce_fusion
  518.0 2.8 fusion.185
  520.8 1.3 slice.188
  522.1 1.1 copy.107
  524.0 1.3 slice.187
  525.3 1.1 copy.106
  527.5 2.1 fusion.80
  (119 shorter events, 23.2 us)
Async XLA Ops:
  7.2 7.8 %copy-start.3 = (f32[2,1,1,4,1,64,512]{6,5,4,3,2,1,0:T(8,128)S(1)}, f32[2,1,1,4,1,64,512]{6,5,4,3,2,1,0:T(8,128)}, u32[]{:S(2)}) copy-start(f32[2,1,1,4,1,64,512]{6,5,4,3,2,1,0:T(8,128)} %param.24) | copy-start | bytes 3145732
  7.2 40.9 %all-gather.4.cloned.1.call-start = ((), (), s32[]{:S(2)}) async-start(), calls=%async_computation.1 | async-start | bytes 3538944 | tf_op jit(solution)/shard_map/all_gather | solution.py:75
  7.9 107.8 %all-gather.6.cloned.1.call-start = ((), (), s32[]{:S(2)}) async-start(), calls=%async_computation.2 | async-start | bytes 3145728 | tf_op jit(solution)/shard_map/all_gather | solution.py:46
  49.7 1.6 slice-start
  73.2 1.8 copy-start
  74.2 214.4 %all-gather.8.cloned.1.call-start = ((), (), s32[]{:S(2)}) async-start(), calls=%async_computation.3 | async-start | bytes 3145728 | tf_op jit(solution)/shard_map/all_gather | solution.py:46
  74.9 3.2 copy-start.4
  79.4 14.7 %copy-start.5 = (bf16[2048,128]{1,0:T(8,128)(2,1)S(1)}, bf16[2048,128]{1,0:T(8,128)(2,1)}, u32[]{:S(2)}) copy-start(bf16[2048,128]{1,0:T(8,128)(2,1)} %copy-done.4) | copy-start | bytes 1572868 | tf_op jit(solution)/shard_map/while
  94.1 3.2 copy-start.4
  98.5 14.7 %copy-start.5 = (bf16[2048,128]{1,0:T(8,128)(2,1)S(1)}, bf16[2048,128]{1,0:T(8,128)(2,1)}, u32[]{:S(2)}) copy-start(bf16[2048,128]{1,0:T(8,128)(2,1)} %copy-done.4) | copy-start | bytes 1572868 | tf_op jit(solution)/shard_map/while
  117.5 6.2 %copy-start.7 = (f32[1,1,1,4,1,64,512]{6,5,4,3,2,1,0:T(8,128)S(1)}, f32[1,1,1,4,1,64,512]{6,5,4,3,2,1,0:T(8,128)}, u32[]{:S(2)}) copy-start(f32[1,1,1,4,1,64,512]{6,5,4,3,2,1,0:T(8,128)} %get-tuple-element.416) | copy-start | bytes 1572868
  126.8 16.0 %copy-start.6 = (f32[1,1,1,4,1,64,512]{6,5,4,3,2,1,0:T(8,128)S(1)}, f32[1,1,1,4,1,64,512]{6,5,4,3,2,1,0:T(8,128)}, u32[]{:S(2)}) copy-start(f32[1,1,1,4,1,64,512]{6,5,4,3,2,1,0:T(8,128)} %get-tuple-element.415) | copy-start | bytes 1572868
  163.0 364.5 %reduce-scatter.2.cloned.1.call-start = ((), (), s32[]{:S(2)}) async-start(), calls=%async_computation.4 | async-start | bytes 3538944 | tf_op jit(solution)/shard_map/reduce_scatter | solution.py:158
  306.0 1.3 copy-start.1
  306.0 1.3 copy-start.2
  307.4 37.7 %collective-permute-start = (f32[12,1,1,512]{3,2,0,1:T(1,128)S(1)}, f32[12,1,1,512]{3,2,0,1:T(1,128)S(1)}, u32[]{:S(2)}, u32[]{:S(2)}) collective-permute-start(f32[12,1,1,512]{3,2,0,1:T(1,128)S(1)} %get-tuple-element.413), channel_id=1, source_target_pairs={{0,1},{1,4},{4,5},{5,8},{8,9},{9,12},{12,13},{2,3},{3,6},{6,7},{7,... | collective-permute-start | bytes 73736 | tf_op jit(solution)/shard_map/ppermute | solution.py:22
  309.6 152.4 %collective-permute-start.1 = (f32[12,1,1,512]{3,2,0,1:T(1,128)S(1)}, f32[12,1,1,512]{3,2,0,1:T(1,128)S(1)}, u32[]{:S(2)}, u32[]{:S(2)}) collective-permute-start(f32[12,1,1,512]{3,2,0,1:T(1,128)S(1)} %get-tuple-element.414), channel_id=1, source_target_pairs={{1,0},{4,1},{5,4},{8,5},{9,8},{12,9},{13,12},{3,2},{6,3},{7,6},{10... | collective-permute-start | bytes 73736 | tf_op jit(solution)/shard_map/ppermute | solution.py:24
  463.9 35.6 %collective-permute-start.3 = (f32[12,1,66,512]{3,1,2,0:T(1,128)S(1)}, f32[12,1,66,512]{3,1,2,0:T(1,128)}, u32[]{:S(2)}, u32[]{:S(2)}) collective-permute-start(f32[12,1,66,512]{3,1,2,0:T(1,128)S(1)} %copy.89), channel_id=1, source_target_pairs={{2,0},{3,1},{6,4},{7,5},{10,8},{11,9},{14,12},{15,13},{18,16},{19,... | collective-permute-start | bytes 4866056 | tf_op jit(solution)/shard_map/ppermute | solution.py:24
  467.6 37.9 %collective-permute-start.2 = (f32[12,1,66,512]{3,1,2,0:T(1,128)S(1)}, f32[12,1,66,512]{3,1,2,0:T(1,128)}, u32[]{:S(2)}, u32[]{:S(2)}) collective-permute-start(f32[12,1,66,512]{3,1,2,0:T(1,128)S(1)} %copy.89), channel_id=1, source_target_pairs={{0,2},{1,3},{4,6},{5,7},{8,10},{9,11},{12,14},{13,15},{16,18},{17,... | collective-permute-start | bytes 4866056 | tf_op jit(solution)/shard_map/ppermute | solution.py:22
Sparse Core Ops, SparseCore 0:
  9.6 38.4 all-gather.3
  74.4 10.6 all-gather.5
  163.2 125.4 all-gather.7
  306.1 184.4 reduce-scatter.1
where the time goes:
time: 544 us; the launch traced here: 536 us
  waiting for transfers between devices  268 us (49%)
  matrix products  79.6 us (15%)
  local copies, waits for them, and re-layouts  64.7 us (12%)
  other arithmetic  62.5 us (11%)
  starting transfers between devices  43.1 us (8%)
  between operations  15.2 us (3%)
    ppermute x2, waiting for transfers between devices, padded(): lax.ppermute(head, axis, [((i + 1) % count, i) for i in range(ends)])  147 us
    all_gather x2, waiting for transfers between devices, pair_rows(): joined = lax.all_gather(pieces, 'rep', axis=2, tiled=True)  83.6 us
    dot_general x16, matrix products, matmul(): jnp.dot(left, right, precision=highest, preferred_element_type=jnp.float32)  78.4 us
    ppermute x2, starting transfers between devices, padded(): lax.ppermute(head, axis, [((i + 1) % count, i) for i in range(ends)])  39.2 us
    all_gather x1, waiting for transfers between devices, on_device(): gathered = lax.all_gather(images, ('view', 'rep'), axis=2, tiled=True)  32.1 us
    scatter-add x2, other arithmetic, forward_block(): return sino_part.at[positions].add(contrib * live_flag)  29.3 us
    gather x2, local copies, waits for them, and re-layouts, back_block(): pet_residual[positions]  26.1 us
  transfers between devices with their start and end apart: 8, of which 5 were waited for; matrix products, arithmetic and copies ran while one was open for 21% of the time, Pallas kernels for 0%

commit v1 on v0

v1 whole, which is shorter than its diff:
```python
import math

import jax
import jax.numpy as jnp
import ml_dtypes
import numpy as np
from jax import lax
from jax.experimental import pallas as pl
from jax.experimental.pallas import tpu as pltpu
from jax.sharding import PartitionSpec as P

kappa = 4.0
step_size = 0.4
penalty = 0.5
bf16 = jnp.bfloat16
f32 = jnp.float32


def contract(left, right, left_dim, right_dim):
    return lax.dot_general(
        left, right, (((left_dim,), (right_dim,)), ((), ())), preferred_element_type=f32
    )


def split_table(table):
    high = table.astype(ml_dtypes.bfloat16)
    low = (table - high.astype(np.float64)).astype(ml_dtypes.bfloat16)
    return high, low


def split_data(values):
    high = values.astype(bf16)
    return high, (values - high.astype(f32)).astype(bf16)


def one_hot(count, index):
    rows = lax.broadcasted_iota(jnp.int32, (count, index.shape[1]), 0)
    return jnp.where(rows == index, 1.0, 0.0).astype(bf16)


def masked_pair(values, ids, pair):
    parts = []
    for which in range(2):
        flag = jnp.where(ids == 2 * pair + which, 1.0, 0.0).astype(bf16)
        parts.append(values * flag)
    return jnp.concatenate(parts, axis=0)


def project_kernel(info_ref, rows_ref, tiles_ref, sino_ref, total):
    local, ids, start = info_ref[0, 0:1], info_ref[0, 1:2], info_ref[0, 2:3]
    tile = tiles_ref.shape[1]
    pixels = contract(rows_ref[...], one_hot(rows_ref.shape[0], local), 0, 0).astype(bf16)
    total[...] = jnp.zeros_like(total)

    def step(pair, carry):
        tiles = jnp.concatenate([tiles_ref[2 * pair], tiles_ref[2 * pair + 1]], axis=1)
        total[...] += contract(tiles, masked_pair(pixels, ids, pair), 1, 0)
        return carry

    lax.fori_loop(0, tiles_ref.shape[0] // 2, step, 0)
    moved = jnp.concatenate([total[...], jnp.zeros_like(total)], axis=0)
    shift = start % tile
    for bit in range(int(math.log2(tile))):
        moved = jnp.where((shift >> bit) & 1 == 1, pltpu.roll(moved, 1 << bit, 0), moved)
    bins = start // tile
    rows = sino_ref.shape[0]

    @pl.when(pl.program_id(0) == 0)
    def _():
        sino_ref[...] = jnp.zeros_like(sino_ref)

    for half in range(2):
        place = one_hot(rows, bins + half)
        rest = moved[half * tile : (half + 1) * tile]
        for _ in range(3):
            part = rest.astype(bf16)
            sino_ref[...] += contract(place, part, 1, 1)
            rest = rest - part.astype(f32)


def back_kernel(info_ref, resid_ref, tiles_ref, back_ref, total):
    local, ids, start = info_ref[0, 0:1], info_ref[0, 1:2], info_ref[0, 2:3]
    tile = tiles_ref.shape[1]
    bins = start // tile
    shift = start % tile
    resid = resid_ref[...]
    moved = jnp.concatenate(
        [contract(resid, one_hot(resid.shape[0], bins + half), 0, 0) for half in range(2)], axis=0
    )
    for bit in range(int(math.log2(tile))):
        moved = jnp.where(
            (shift >> bit) & 1 == 1, pltpu.roll(moved, 2 * tile - (1 << bit), 0), moved
        )
    window = moved[:tile].astype(bf16)
    total[...] = jnp.zeros_like(total)

    def step(pair, carry):
        tiles = jnp.concatenate([tiles_ref[2 * pair], tiles_ref[2 * pair + 1]], axis=0)
        total[...] += contract(tiles, masked_pair(window, ids, pair), 0, 0)
        return carry

    lax.fori_loop(0, tiles_ref.shape[0] // 2, step, 0)

    @pl.when(pl.program_id(0) == 0)
    def _():
        back_ref[...] = jnp.zeros_like(back_ref)

    place = one_hot(back_ref.shape[0], local)
    rest = total[...]
    for _ in range(3):
        part = rest.astype(bf16)
        back_ref[...] += contract(place, part, 1, 1)
        rest = rest - part.astype(f32)


def tile_call(kernel, info, values, tiles, rows):
    chunks, _, chunk = info.shape
    tile = tiles.shape[1]
    return pl.pallas_call(
        kernel,
        grid=(chunks,),
        out_shape=jax.ShapeDtypeStruct((rows, tile), f32),
        in_specs=[
            pl.BlockSpec((1, 8, chunk), lambda i: (i, 0, 0)),
            pl.BlockSpec(values.shape, lambda i: (0, 0)),
            pl.BlockSpec(tiles.shape, lambda i: (0, 0, 0)),
        ],
        out_specs=pl.BlockSpec((rows, tile), lambda i: (0, 0)),
        scratch_shapes=[pltpu.VMEM((tile, chunk), f32)],
        compiler_params=pltpu.CompilerParams(vmem_limit_bytes=32 * 1024 * 1024),
        cost_estimate=pl.CostEstimate(
            flops=2 * chunks * chunk * tiles.size, bytes_accessed=2 * tiles.size, transcendentals=0
        ),
    )(info, values, tiles)


def on_device(
    images,
    scaled_duals,
    proj_tiles,
    tile_ids,
    pixel_blocks,
    tof_offsets,
    counts,
    sinogram,
    coil_maps,
    kspace,
    sampling,
):
    rep_count = lax.axis_size("rep")
    owner_count = lax.axis_size("view") * rep_count
    slab_count = lax.axis_size("slab")
    rep_at = lax.axis_index("rep")
    slab_at = lax.axis_index("slab")
    owner_at = lax.axis_index("view") * rep_count + rep_at
    row_block = images.shape[2]
    width = images.shape[3]
    tile_size = proj_tiles.shape[1]
    sectors, capacity = tile_ids.shape
    sector_bins = sinogram.shape[1] // sectors
    groups = coil_maps.shape[3]

    own_images = images[:, 0]
    ring = [(i, i + 1) for i in range(owner_count - 1)]
    row_after = lax.ppermute(own_images[:, :1], ("view", "rep"), [(b, a) for a, b in ring])
    chain = [(i, i + 1) for i in range(slab_count - 1)]
    slice_after = lax.ppermute(own_images, "slab", [(b, a) for a, b in chain])

    gathered = lax.all_gather(images[1:3, 0], "view", axis=1, tiled=True)
    own_image = gathered.reshape(2, groups * row_block, width)

    own_blocks = row_block * width // tile_size
    local = pixel_blocks - owner_at * own_blocks
    live = jnp.arange(capacity, dtype=jnp.int32)[None] < counts[:, None]
    local = jnp.where(live & (local >= 0) & (local < own_blocks), local, -1)
    start = tof_offsets + sector_bins * jnp.arange(sectors, dtype=jnp.int32)[:, None]
    chunk = 4 * capacity
    lists = [part.reshape(-1, 1, chunk) for part in (local, tile_ids, start)]
    info = jnp.concatenate(lists + [jnp.zeros_like(lists[0])] * 5, axis=1)
    pixel_rows = own_images[0].astype(bf16).reshape(-1, tile_size)
    bin_rows = sinogram.shape[1] // tile_size
    projected = tile_call(project_kernel, info, pixel_rows, proj_tiles, bin_rows)
    full_sino = lax.psum(projected, ("view", "rep"))
    measured = sinogram[0].reshape(bin_rows, tile_size).astype(f32)
    pet_residual = (full_sino - measured).astype(bf16)
    pet_term = tile_call(back_kernel, info, pet_residual, proj_tiles, own_blocks)
    pet_term = pet_term.reshape(row_block, width)

    grid = np.arange(width)
    angle = (np.outer(grid, grid) % width) * (2.0 * np.pi / width)
    cosine, sine = np.cos(angle) / np.sqrt(width), np.sin(angle) / np.sqrt(width)
    by_rep = grid.reshape(groups, rep_count, row_block).transpose(1, 0, 2).reshape(rep_count, -1)
    rep_major = by_rep.reshape(-1)
    row_tables = np.stack(
        [
            np.concatenate([table[rows][:, rep_major] for table in (cosine, sine)], axis=0)
            for rows in by_rep
        ]
    )
    row_high, row_low = (
        lax.dynamic_index_in_dim(jnp.asarray(part), rep_at, keepdims=False)
        for part in split_table(row_tables)
    )
    forward = np.block([[cosine, -sine], [sine, cosine]])
    inverse = np.block([[cosine, sine], [-sine, cosine]])

    def columns(real, imag, table):
        high, low = split_data(jnp.concatenate([real, imag], axis=1))
        table_high, table_low = (jnp.asarray(part) for part in split_table(table))
        return (
            contract(high, table_high, 1, 0)
            + contract(low, table_high, 1, 0)
            + contract(high, table_low, 1, 0)
        )

    def rows(values):
        both = lax.all_gather(values, "rep", axis=0, tiled=True)
        high, low = split_data(both)
        out = (
            contract(row_high, high, 1, 0)
            + contract(row_high, low, 1, 0)
            + contract(row_low, high, 1, 0)
        )
        half = out.shape[0] // 2
        return (
            out[:half, :width],
            out[:half, width:],
            out[half:, :width],
            out[half:, width:],
        )

    sens = coil_maps.reshape(2, groups * row_block, width)
    coil_re = sens[0] * own_image[0] - sens[1] * own_image[1]
    coil_im = sens[0] * own_image[1] + sens[1] * own_image[0]
    cos_re, cos_im, sin_re, sin_im = rows(columns(coil_re, coil_im, forward))
    measured_k = kspace.reshape(2, groups * row_block, width)
    acquired = sampling.reshape(-1).astype(f32)[:, None]
    resid_re = acquired * (cos_re + sin_im - measured_k[0])
    resid_im = acquired * (cos_im - sin_re - measured_k[1])
    cos_re, cos_im, sin_re, sin_im = rows(columns(resid_re, resid_im, inverse))
    image_re = cos_re - sin_im
    image_im = cos_im + sin_re
    grad_re = sens[0] * image_re + sens[1] * image_im
    grad_im = sens[0] * image_im - sens[1] * image_re
    coil_rows = jnp.stack([grad_re, grad_im]).reshape(2, groups, row_block, width)
    coil_gradient = lax.psum_scatter(coil_rows, "view", scatter_dimension=1, tiled=True)
    data_gradient = jnp.concatenate([pet_term[None], coil_gradient[:, 0]], axis=0)

    global_rows = owner_at * row_block + jnp.arange(row_block, dtype=jnp.int32)
    row_keep = (global_rows < width - 1).astype(f32)[None, :, None]
    slice_keep = (slab_at < slab_count - 1).astype(f32)
    column_keep = (jnp.arange(width) < width - 1).astype(f32)[None, None, :]
    next_row = jnp.concatenate([own_images[:, 1:], row_after], axis=1)
    next_column = jnp.concatenate([own_images[..., 1:], own_images[..., :1]], axis=-1)
    diff_rows = (next_row - own_images) * row_keep
    diff_columns = (next_column - own_images) * column_keep
    diff_slices = (slice_after - own_images) * slice_keep
    differences = jnp.stack([diff_rows, diff_columns, diff_slices], axis=1).reshape(
        9, row_block, width
    )
    spread = differences + scaled_duals[:, 0]
    magnitude = jnp.sqrt(jnp.sum(spread * spread, axis=0))
    shrunk = spread * (jnp.maximum(magnitude - kappa, 0.0) / jnp.maximum(magnitude, kappa))[None]
    dual_next = spread - shrunk
    coupling = (differences - shrunk + dual_next).reshape(3, 3, row_block, width)
    couple_rows = coupling[:, 0] * row_keep
    couple_columns = coupling[:, 1] * column_keep
    couple_slices = coupling[:, 2] * slice_keep
    row_before = lax.ppermute(couple_rows[:, -1:], ("view", "rep"), ring)
    slice_before = lax.ppermute(couple_slices, "slab", chain)
    adjoint = (
        jnp.concatenate([row_before, couple_rows[:, :-1]], axis=1)
        - couple_rows
        + jnp.concatenate([couple_columns[..., -1:], couple_columns[..., :-1]], axis=-1)
        - couple_columns
        + slice_before
        - couple_slices
    )
    updated = own_images - step_size * (data_gradient + penalty * adjoint)
    return (updated[:, None], shrunk[:, None], dual_next[:, None])


def solution(mesh):
    placed = (
        P(None, ("grp", "slab"), ("view", "rep"), None),
        P(None, ("grp", "slab"), ("view", "rep"), None),
        P(),
        P(),
        P(),
        P(),
        P(),
        P(("grp", "slab"), None),
        P(None, "view", ("grp", "slab"), None, "rep", None, None),
        P(None, "view", ("grp", "slab"), None, "rep", None, None),
        P(("grp", "slab"), None, "rep", None),
    )
    return jax.shard_map(
        on_device,
        mesh=mesh,
        in_specs=placed,
        out_specs=(
            P(None, ("grp", "slab"), ("view", "rep"), None),
            P(None, ("grp", "slab"), ("view", "rep"), None),
            P(None, ("grp", "slab"), ("view", "rep"), None),
        ),
        check_vma=False,
    )
```

time: 544 us -> 157 us (0.29)
  the two profiles are of different devices: /device:TPU:10 before, /device:TPU:0 now
where the time goes in v1:
time: 157 us
  waiting for transfers between devices  51.1 us (33%)
  blocking collectives  29.3 us (19%)
  Pallas kernels  14.8 us (9%)
  between operations  14.2 us (9%)
  matrix products  14.1 us (9%)
  local copies, waits for them, and re-layouts  12.9 us (8%)
  other arithmetic  11.9 us (8%)
  starting transfers between devices  8.29 us (5%)
    all_gather x1, waiting for transfers between devices, on_device(): gathered = lax.all_gather(images[1:3, 0], 'view', axis=1, tiled=True)  30.5 us
    psum x1, blocking collectives, on_device(): full_sino = lax.psum(projected, ('view', 'rep'))  29.3 us
    pallas_call x2, Pallas kernels, tile_call(): pl.pallas_call(kernel, grid=(chunks,), out_shape=jax.ShapeDtypeStruct((ro...  14.8 us
    reduce_scatter x1, waiting for transfers between devices, on_device(): lax.psum_scatter(coil_rows, 'view', scatter_dimension=1, tiled=True)  14.8 us
    dot_general x12, matrix products, contract(): lax.dot_general(left, right, (((left_dim,), (right_dim,)), ((), ())), pre...  14.1 us
    unnamed x42, local copies, waits for them, and re-layouts  4.68 us
    all_gather x2, waiting for transfers between devices, rows(): both = lax.all_gather(values, 'rep', axis=0, tiled=True)  4.53 us
    ppermute x1, starting transfers between devices, on_device(): slice_before = lax.ppermute(couple_slices, 'slab', chain)  4.14 us
  transfers between devices with their start and end apart: 8, of which 4 were waited for; matrix products, arithmetic and copies ran while one was open for 13% of the time, Pallas kernels for 9%

profile of v1, /device:TPU:0, one launch (start us, length us, event | category | flops | bytes accessed | tf_op | source)
XLA Modules:
  0.0 156.7 jit_solution(6534163411728612081)
XLA Ops:
  7.2 0.0 all-gather.9.cloned.1.call-start
  7.2 1.7 %slice.97 = f32[2,1,64,512]{3,2,1,0:T(8,128)} slice(f32[3,1,64,512]{3,2,1,0:T(8,128)} %param.17), slice={[1:3], [0:1], [0:64], [0:512]} | slice | bytes 524288 | tf_op jit(solution)/shard_map/slice | solution.py:169
  8.9 0.0 all-gather.9.cloned.1.call-update
  8.9 0.0 all-gather.5.cloned.1.call-start
  9.0 1.3 fusion.72
  10.3 30.5 %all-gather.9.cloned.1.call-done = f32[2,1,256,512]{3,2,1,0:T(8,128)} async-done(((f32[2,1,64,512]{3,2,1,0:T(8,128)}), f32[2,1,256,512]{3,2,1,0:T(8,128)}) %all-gather.9.cloned.1.call-update) | async-done | bytes 1048592 | tf_op jit(solution)/shard_map/all_gather | solution.py:169
  40.8 1.4 fusion.13
  42.2 0.7 fusion.42
  43.0 0.8 convolution_add_fusion.3
  43.8 0.8 copy-done.11
  44.6 1.7 %convolution_add_fusion.2 = f32[256,1024]{1,0:T(8,128)} fusion(f32[256,1024]{1,0:T(8,128)S(1)} %convolution_add_fusion.3, bf16[1024,1024]{1,0:T(8,128)(2,1)S(1)} %copy-done.11, f32[256,512]{1,0:T(8,128)S(1)} %get-tuple-element.18, f32[256,512]{1,0:T(8,128)S(1)} %get-tuple-element.17), kind=kOutput, calls=%fused_computation.8 | convolution fusion | flops 538181632 | bytes 5242880 | tf_op jit(solution)/shard_map/dot_general | solution.py:20
  46.3 0.0 all-gather.5.cloned.1.call-update
  46.3 0.0 all-gather.7.cloned.1.call-start
  46.4 1.4 collective-permute-start.1
  47.8 0.6 slice.136
  48.4 1.3 collective-permute-start
  49.8 0.1 convert_element_type.84
  49.8 0.1 broadcast_add_fusion
  50.0 0.1 fusion.50
  50.1 0.6 pad.22.clone
  50.7 1.4 fusion.71
  52.0 4.5 %all-gather.5.cloned.1.call-done = f32[512,1024]{1,0:T(8,128)} async-done(((f32[256,1024]{1,0:T(8,128)}), f32[512,1024]{1,0:T(8,128)}) %all-gather.5.cloned.1.call-update) | async-done | bytes 2097168 | tf_op jit(solution)/shard_map/all_gather | solution.py:217
  56.6 2.4 %fusion.21 = f32[512,1024]{1,0:T(8,128)S(1)} fusion(bf16[2,512,512]{2,1,0:T(8,128)(2,1)S(1)} %copy-done.7, s32[]{:T(128)S(6)} %select_n.10, f32[512,1024]{1,0:T(8,128)} %all-gather.5.cloned.1.call-done), kind=kOutput, calls=%fused_computation.53 | convolution fusion | flops 537395200 | bytes 4718596 | tf_op jit(solution)/shard_map/dot_general | solution.py:20
  59.0 0.7 fusion.1
  59.8 0.5 copy-done.12
  60.3 0.8 add_add_fusion.1
  61.0 0.2 fusion.8
  61.3 1.4 copy-done.5
  62.6 0.7 fusion.46
  63.3 0.7 convolution_add_fusion.1
  64.1 0.9 copy-done.10
  64.9 1.7 %convolution_add_fusion = f32[256,1024]{1,0:T(8,128)} fusion(f32[256,1024]{1,0:T(8,128)S(1)} %convolution_add_fusion.1, bf16[1024,1024]{1,0:T(8,128)(2,1)S(1)} %copy-done.10, f32[256,512]{1,0:T(8,128)S(1)} %get-tuple-element.16, f32[256,512]{1,0:T(8,128)S(1)} %get-tuple-element.15), kind=kOutput, calls=%fused_computation.6 | convolution fusion | flops 538181632 | bytes 5242880 | tf_op jit(solution)/shard_map/dot_general | solution.py:20
  66.7 0.0 reduce-scatter.2.cloned.1.call-start
  66.7 0.1 add_add_fusion.2.info_ref
  66.8 0.1 convert_element_type.79.rows_ref
  66.9 7.2 %shard_map.184 = f32[64,128]{1,0:T(8,128)S(1)} custom-call(s32[1,8,1024]{2,1,0:T(8,128)S(1)} %add_add_fusion.2.info_ref, bf16[256,128]{1,0:T(8,128)(2,1)S(1)} %convert_element_type.79.rows_ref, bf16[48,128,128]{2,1,0:T(8,128)(2,1)S(1)} %copy-done), custom_call_target="tpu_custom_call" | custom-call | flops 1610612736 | bytes 1572864 | tf_op jit(solution)/shard_map/pallas_call | solution.py:119
  74.1 29.3 %psum.7 = f32[64,128]{1,0:T(8,128)S(1)} all-reduce(f32[64,128]{1,0:T(8,128)S(1)} %shard_map.184), channel_id=1, replica_groups=mesh['grp'=2,'view'=4,'slab'=2,'rep'=2] {'view','rep'}, use_global_device_ids=true, to_apply=%region_0.1 | all-reduce | flops 8192 | bytes 65536 | tf_op jit(solution)/shard_map/psum | solution.py:183
  103.4 7.6 %shard_map.185 = f32[256,128]{1,0:T(8,128)S(1)} custom-call(s32[1,8,1024]{2,1,0:T(8,128)S(1)} %add_add_fusion.2.info_ref, bf16[64,128]{1,0:T(8,128)(2,1)S(1)} %subtract_convert_fusion.8.resid_ref, bf16[48,128,128]{2,1,0:T(8,128)(2,1)S(1)} %copy-done), custom_call_target="tpu_custom_call" | custom-call | flops 1610612736 | bytes 1572864 | tf_op jit(solution)/shard_map/pallas_call | solution.py:119
  111.1 0.8 slice_bitcast_fusion.5
  111.8 0.9 slice_bitcast_fusion.4
  112.8 0.7 broadcast_in_dim_reshape.3
  113.4 1.3 fusion.33
  114.7 1.8 %multiply_bitcast_fusion.1 = f32[3,1,64,512]{3,2,0,1:T(8,128)} fusion(f32[3,64,512]{2,1,0:T(8,128)} %collective-permute-done.1, f32[]{:T(128)S(6)} %convert_element_type.99, f32[3,1,64,512]{3,2,1,0:T(8,128)S(1)} %copy-done.3), kind=kLoop, calls=%fused_computation.85 | loop fusion | flops 196608 | bytes 1179652 | tf_op jit(solution)/shard_map/stack | solution.py:258
  116.5 2.5 %fusion.18 = f32[512,1024]{1,0:T(8,128)S(1)} fusion(bf16[2,512,512]{2,1,0:T(8,128)(2,1)S(1)} %copy-done.8, s32[]{:T(128)S(6)} %select_n.10, f32[512,1024]{1,0:T(8,128)} %all-gather.7.cloned.1.call-done), kind=kOutput, calls=%fused_computation.50 | convolution fusion | flops 537395200 | bytes 4718596 | tf_op jit(solution)/shard_map/dot_general | solution.py:20
  119.0 0.7 fusion.2
  119.7 0.5 copy-done.13
  120.2 0.7 add_add_fusion
  121.0 0.4 fusion.15
  121.4 1.1 pad_maximum_fusion.3
  122.5 0.5 copy-done.4
  123.0 0.1 copy-done.9
  123.1 0.3 bitcast_add_fusion.1
  123.4 0.3 multiply_reduce_fusion
  123.7 0.1 maximum_divide_fusion
  123.7 0.3 fusion.70
  124.1 0.4 copy_add_fusion
  124.5 4.1 %collective-permute-start.3 = (f32[3,64,512]{2,1,0:T(8,128)S(1)}, f32[3,64,512]{2,1,0:T(8,128)}, u32[]{:S(2)}, u32[]{:S(2)}) collective-permute-start(f32[3,64,512]{2,1,0:T(8,128)S(1)} %fusion.27), channel_id=1, source_target_pairs={{0,2},{1,3},{4,6},{5,7},{8,10},{9,11},{12,14},{13,15},{16,18},{17,... | collective-permute-start | bytes 1179656 | tf_op jit(solution)/shard_map/ppermute | solution.py:270
  128.6 0.1 fusion.29
  128.8 1.3 collective-permute-start.2
  130.1 1.8 %fusion = (f32[9,1,64,512]{3,2,1,0:T(8,128)}, f32[9,1,64,512]{3,2,1,0:T(8,128)}) fusion(f32[64,512]{1,0:T(8,128)S(1)} %maximum_divide_fusion, f32[9,1,64,512]{3,2,1,0:T(8,128)S(1)} %copy-done.4, f32[3,3,64,512]{3,2,1,0:T(8,128)S(1)} %get-tuple-element.22), kind=kLoop, calls=%fused_computation.10 | loop fusion | flops 884736 | bytes 4849664
  131.9 0.1 slice.143
  132.0 1.2 collective-permute-done.3
  133.2 14.8 %reduce-scatter.2.cloned.1.call-done = f32[2,1,64,512]{3,2,0,1:T(8,128)} async-done(((f32[2,4,64,512]{3,2,0,1:T(8,128)}), f32[2,1,64,512]{3,2,0,1:T(8,128)}) %reduce-scatter.2.cloned.1.call-update) | async-done | bytes 262160 | tf_op jit(solution)/shard_map/reduce_scatter | solution.py:246
  147.9 2.2 %fusion.32 = f32[3,1,64,512]{3,2,1,0:T(8,128)} fusion(f32[2,64,512]{2,1,0:T(8,128)} %bitcast.143, f32[1,64,512]{2,1,0:T(8,128)} %broadcast_in_dim_reshape.3, f32[3,64,512]{2,1,0:T(8,128)} %collective-permute-done.3, f32[3,64,512]{2,1,0:T(8,128)S(1)} %get-tuple-element.20, f32[3,64,512]{2,1,0:T(8,128)S(1)} %get-tuple-element.19, ...), kind=kLoop, calls=%fused_computation.74 | loop fusion | flops 1277952 | bytes 3538948
  (55 shorter events, 0.3 us)
Async XLA Ops:
  7.2 33.6 %all-gather.9.cloned.1.call-start = ((), (), s32[]{:S(2)}) async-start(), calls=%async_computation.4 | async-start | bytes 1310720 | tf_op jit(solution)/shard_map/all_gather | solution.py:169
  8.9 47.6 %all-gather.5.cloned.1.call-start = ((), (), s32[]{:S(2)}) async-start(), calls=%async_computation.1 | async-start | bytes 3145728 | tf_op jit(solution)/shard_map/all_gather | solution.py:217
  10.3 32.0 %copy-start.6 = (bf16[1024,1024]{1,0:T(8,128)(2,1)S(1)}, bf16[1024,1024]{1,0:T(8,128)(2,1)}, u32[]{:S(2)}) copy-start(bf16[1024,1024]{1,0:T(8,128)(2,1)} %constant.61.clone) | copy-start | bytes 6291460
  43.0 1.6 %copy-start.11 = (bf16[1024,1024]{1,0:T(8,128)(2,1)S(1)}, bf16[1024,1024]{1,0:T(8,128)(2,1)}, u32[]{:S(2)}) copy-start(bf16[1024,1024]{1,0:T(8,128)(2,1)} %constant.62.clone) | copy-start | bytes 6291460
  44.6 1.8 %copy-start.3 = (f32[3,1,64,512]{3,2,1,0:T(8,128)S(1)}, f32[3,1,64,512]{3,2,1,0:T(8,128)}, u32[]{:S(2)}) copy-start(f32[3,1,64,512]{3,2,1,0:T(8,128)} %param.17) | copy-start | bytes 1179652
  44.6 5.1 %copy-start.18 = (s32[1,4,1,64]{3,2,1,0:T(1,128)S(1)}, s32[1,4,1,64]{3,2,1,0:T(1,128)}, u32[]{:S(2)}) copy-start(s32[1,4,1,64]{3,2,1,0:T(1,128)} %param.27) | copy-start | bytes 3076
  44.6 5.3 %copy-start.15 = (s32[4,256]{1,0:T(4,128)S(1)}, s32[4,256]{1,0:T(4,128)}, u32[]{:S(2)}) copy-start(s32[4,256]{1,0:T(4,128)} %param.22) | copy-start | bytes 12292
  44.6 5.3 %copy-start.16 = (s32[4,256]{1,0:T(4,128)S(1)}, s32[4,256]{1,0:T(4,128)}, u32[]{:S(2)}) copy-start(s32[4,256]{1,0:T(4,128)} %param.20) | copy-start | bytes 12292
  44.6 5.4 %copy-start.17 = (s32[4,256]{1,0:T(4,128)S(1)}, s32[4,256]{1,0:T(4,128)}, u32[]{:S(2)}) copy-start(s32[4,256]{1,0:T(4,128)} %param.21) | copy-start | bytes 12292
  44.6 5.4 %copy-start.20 = (s32[4]{0:T(128)S(1)}, s32[4]{0:T(128)}, u32[]{:S(2)}) copy-start(s32[4]{0:T(128)} %param.23) | copy-start | bytes 52
  46.3 10.3 %copy-start.7 = (bf16[2,512,512]{2,1,0:T(8,128)(2,1)S(1)}, bf16[2,512,512]{2,1,0:T(8,128)(2,1)}, u32[]{:S(2)}) copy-start(bf16[2,512,512]{2,1,0:T(8,128)(2,1)} %constant.59.clone) | copy-start | bytes 3145732
  46.3 70.2 %all-gather.7.cloned.1.call-start = ((), (), s32[]{:S(2)}) async-start(), calls=%async_computation.2 | async-start | bytes 3145728 | tf_op jit(solution)/shard_map/all_gather | solution.py:217
  46.4 68.3 %collective-permute-start.1 = (f32[3,64,512]{2,1,0:T(8,128)S(1)}, f32[3,64,512]{2,1,0:T(8,128)}, u32[]{:S(2)}, u32[]{:S(2)}) collective-permute-start(f32[3,64,512]{2,1,0:T(8,128)S(1)} %bitcast.133), channel_id=1, source_target_pairs={{2,0},{3,1},{6,4},{7,5},{10,8},{11,9},{14,12},{15,13},{18,16},{19,... | collective-permute-start | bytes 1179656 | tf_op jit(solution)/shard_map/ppermute | solution.py:167
  48.4 65.0 %collective-permute-start = (f32[3,1,512]{2,1,0:T(1,128)}, f32[3,1,512]{2,1,0:T(1,128)}, u32[]{:S(2)}, u32[]{:S(2)}) collective-permute-start(f32[3,1,512]{2,1,0:T(1,128)} %slice.136), channel_id=1, source_target_pairs={{1,0},{4,1},{5,4},{8,5},{9,8},{12,9},{13,12},{3,2},{6,3},{7,6},{10... | collective-permute-start | bytes 18440 | tf_op jit(solution)/shard_map/ppermute | solution.py:165
  56.6 2.5 %copy-start.2 = (f32[512,1024]{1,0:T(8,128)S(1)}, f32[512,1024]{1,0:T(8,128)}, u32[]{:S(2)}) copy-start(f32[512,1024]{1,0:T(8,128)} %all-gather.5.cloned.1.call-done) | copy-start | bytes 6291460
  59.0 1.2 copy-start.12
  61.0 1.6 %copy-start.5 = (bf16[1024,1024]{1,0:T(8,128)(2,1)S(1)}, bf16[1024,1024]{1,0:T(8,128)(2,1)}, u32[]{:S(2)}) copy-start(bf16[1024,1024]{1,0:T(8,128)(2,1)} %constant.63.clone) | copy-start | bytes 6291460
  63.3 1.6 %copy-start.10 = (bf16[1024,1024]{1,0:T(8,128)(2,1)S(1)}, bf16[1024,1024]{1,0:T(8,128)(2,1)}, u32[]{:S(2)}) copy-start(bf16[1024,1024]{1,0:T(8,128)(2,1)} %constant.64.clone) | copy-start | bytes 6291460
  64.9 1.8 %copy-start.19 = (s32[8]{0:T(128)S(1)}, s32[8]{0:T(128)}, u32[]{:S(2)}) copy-start(s32[8]{0:T(128)} %pad.22.clone) | copy-start | bytes 100
  64.9 1.9 %copy-start.14 = (bf16[1,8192]{1,0:T(2,128)(2,1)S(1)}, bf16[1,8192]{1,0:T(2,128)(2,1)}, u32[]{:S(2)}) copy-start(bf16[1,8192]{1,0:T(2,128)(2,1)} %param.24) | copy-start | bytes 49156
  64.9 2.0 %copy-start = (bf16[48,128,128]{2,1,0:T(8,128)(2,1)S(1)}, bf16[48,128,128]{2,1,0:T(8,128)(2,1)}, u32[]{:S(2)}) copy-start(bf16[48,128,128]{2,1,0:T(8,128)(2,1)} %tiles_ref.3) | copy-start | bytes 4718596
  66.7 81.3 %reduce-scatter.2.cloned.1.call-start = ((), (), s32[]{:S(2)}) async-start(), calls=%async_computation.3 | async-start | bytes 1310720 | tf_op jit(solution)/shard_map/reduce_scatter | solution.py:246
  111.8 4.7 %copy-start.8 = (bf16[2,512,512]{2,1,0:T(8,128)(2,1)S(1)}, bf16[2,512,512]{2,1,0:T(8,128)(2,1)}, u32[]{:S(2)}) copy-start(bf16[2,512,512]{2,1,0:T(8,128)(2,1)} %constant.59.clone) | copy-start | bytes 3145732
  116.5 2.5 %copy-start.1 = (f32[512,1024]{1,0:T(8,128)S(1)}, f32[512,1024]{1,0:T(8,128)}, u32[]{:S(2)}) copy-start(f32[512,1024]{1,0:T(8,128)} %all-gather.7.cloned.1.call-done) | copy-start | bytes 6291460
  119.0 1.2 copy-start.13
  121.3 1.7 %copy-start.4 = (f32[9,1,64,512]{3,2,1,0:T(8,128)S(1)}, f32[9,1,64,512]{3,2,1,0:T(8,128)}, u32[]{:S(2)}) copy-start(f32[9,1,64,512]{3,2,1,0:T(8,128)} %param.18) | copy-start | bytes 3538948
  121.3 1.7 %copy-start.9 = (f32[3,1,64,512]{3,2,0,1:T(8,128)S(1)}, f32[3,1,64,512]{3,2,0,1:T(8,128)}, u32[]{:S(2)}) copy-start(f32[3,1,64,512]{3,2,0,1:T(8,128)} %multiply_bitcast_fusion.1) | copy-start | bytes 1179652
  124.5 8.7 %collective-permute-start.3 = (f32[3,64,512]{2,1,0:T(8,128)S(1)}, f32[3,64,512]{2,1,0:T(8,128)}, u32[]{:S(2)}, u32[]{:S(2)}) collective-permute-start(f32[3,64,512]{2,1,0:T(8,128)S(1)} %fusion.27), channel_id=1, source_target_pairs={{0,2},{1,3},{4,6},{5,7},{8,10},{9,11},{12,14},{13,15},{16,18},{17,... | collective-permute-start | bytes 1179656 | tf_op jit(solution)/shard_map/ppermute | solution.py:270
  128.8 3.2 %collective-permute-start.2 = (f32[3,1,512]{2,1,0:T(1,128)S(1)}, f32[3,1,512]{2,1,0:T(1,128)S(1)}, u32[]{:S(2)}, u32[]{:S(2)}) collective-permute-start(f32[3,1,512]{2,1,0:T(1,128)S(1)} %slice.140), channel_id=1, source_target_pairs={{0,1},{1,4},{4,5},{5,8},{8,9},{9,12},{12,13},{2,3},{3,6},{6,7},{7,... | collective-permute-start | bytes 18440 | tf_op jit(solution)/shard_map/ppermute | solution.py:269
Sparse Core Ops, SparseCore 0:
  10.1 30.6 all-gather.8
  46.5 10.0 all-gather.4
  66.8 11.7 all-gather.6
  122.6 25.2 reduce-scatter.1

commit v2 on v1

--- a/solution.py
+++ b/solution.py
@@ -1,3 +1,4 @@
+import functools
 import math
 
 import jax
@@ -46,8 +47,8 @@
     return jnp.concatenate(parts, axis=0)
 
 
-def project_kernel(info_ref, rows_ref, tiles_ref, sino_ref, total):
-    local, ids, start = info_ref[0, 0:1], info_ref[0, 1:2], info_ref[0, 2:3]
+def project(info_ref, at, rows_ref, tiles_ref, sino_ref, total):
+    local, ids, start = info_ref[at, 0:1], info_ref[at, 1:2], info_ref[at, 2:3]
     tile = tiles_ref.shape[1]
     pixels = contract(rows_ref[...], one_hot(rows_ref.shape[0], local), 0, 0).astype(bf16)
     total[...] = jnp.zeros_like(total)
@@ -64,11 +65,6 @@
         moved = jnp.where((shift >> bit) & 1 == 1, pltpu.roll(moved, 1 << bit, 0), moved)
     bins = start // tile
     rows = sino_ref.shape[0]
-
-    @pl.when(pl.program_id(0) == 0)
-    def _():
-        sino_ref[...] = jnp.zeros_like(sino_ref)
-
     for half in range(2):
         place = one_hot(rows, bins + half)
         rest = moved[half * tile : (half + 1) * tile]
@@ -78,12 +74,11 @@
             rest = rest - part.astype(f32)
 
 
-def back_kernel(info_ref, resid_ref, tiles_ref, back_ref, total):
-    local, ids, start = info_ref[0, 0:1], info_ref[0, 1:2], info_ref[0, 2:3]
+def back_project(info_ref, at, resid, tiles_ref, back_ref, total):
+    local, ids, start = info_ref[at, 0:1], info_ref[at, 1:2], info_ref[at, 2:3]
     tile = tiles_ref.shape[1]
     bins = start // tile
     shift = start % tile
-    resid = resid_ref[...]
     moved = jnp.concatenate(
         [contract(resid, one_hot(resid.shape[0], bins + half), 0, 0) for half in range(2)], axis=0
     )
@@ -100,11 +95,6 @@
         return carry
 
     lax.fori_loop(0, tiles_ref.shape[0] // 2, step, 0)
-
-    @pl.when(pl.program_id(0) == 0)
-    def _():
-        back_ref[...] = jnp.zeros_like(back_ref)
-
     place = one_hot(back_ref.shape[0], local)
     rest = total[...]
     for _ in range(3):
@@ -113,25 +103,268 @@
         rest = rest - part.astype(f32)
 
 
-def tile_call(kernel, info, values, tiles, rows):
-    chunks, _, chunk = info.shape
+MESH = pl.DeviceIdType.MESH
+
+
+def remote(source, target, send_sem, recv_sem, device):
+    return pltpu.make_async_remote_copy(
+        src_ref=source,
+        dst_ref=target,
+        send_sem=send_sem,
+        recv_sem=recv_sem,
+        device_id=device,
+        device_id_type=MESH,
+    )
+
+
+def greet(devices):
+    barrier = pltpu.get_barrier_semaphore()
+    for device in devices:
+        pl.semaphore_signal(barrier, inc=1, device_id=device, device_id_type=MESH)
+    pl.semaphore_wait(barrier, len(devices))
+
+
+def gather_kernel(
+    views,
+    reps,
+    info_ref,
+    rows_ref,
+    tiles_ref,
+    measured_ref,
+    own_ref,
+    gathered_ref,
+    back_ref,
+    total,
+    sino,
+    slots,
+    send_rows,
+    recv_rows,
+    send_sino,
+    recv_sino,
+):
+    view, rep = lax.axis_index("view"), lax.axis_index("rep")
+    count = views * reps
+    me = view * reps + rep
+
+    def owner(index):
+        index = lax.rem(index, count)
+        return {"view": index // reps, "rep": lax.rem(index, reps)}
+
+    greet([owner(me + step) for step in range(1, count)])
+    copies = []
+    for step in range(1, views):
+        device = {"view": lax.rem(view + step, views), "rep": rep}
+        copy = remote(
+            own_ref, gathered_ref.at[view], send_rows.at[step], recv_rows.at[step], device
+        )
+        copy.start()
+        copies.append(copy)
+    gathered_ref[view] = own_ref[...]
+    sino[...] = jnp.zeros_like(sino)
+    for at in range(info_ref.shape[0]):
+        project(info_ref, at, rows_ref, tiles_ref, sino, total)
+    sums = []
+    for step in range(1, count):
+        copy = remote(
+            sino, slots.at[step], send_sino.at[step], recv_sino.at[step], owner(me + step)
+        )
+        copy.start()
+        sums.append(copy)
+    for copy in sums:
+        copy.wait()
+    full = sino[...]
+    for step in range(1, count):
+        full = full + slots[step]
+    resid = (full - measured_ref[...].astype(f32)).astype(bf16)
+    back_ref[...] = jnp.zeros_like(back_ref)
+    for at in range(info_ref.shape[0]):
+        back_project(info_ref, at, resid, tiles_ref, back_ref, total)
+    for step in range(1, views):
+        source = lax.rem(view + views - step, views)
+        remote(
+            own_ref,
+            gathered_ref.at[source],
+            send_rows.at[step],
+            recv_rows.at[step],
+            {"view": source, "rep": rep},
+        ).wait_recv()
+    for copy in copies:
+        copy.wait_send()
+
+
+def gather_call(views, reps, info, rows, tiles, measured, own):
+    chunk = info.shape[2]
     tile = tiles.shape[1]
+    vmem = pl.BlockSpec(memory_space=pltpu.VMEM)
+    dma = pltpu.SemaphoreType.DMA
     return pl.pallas_call(
-        kernel,
-        grid=(chunks,),
-        out_shape=jax.ShapeDtypeStruct((rows, tile), f32),
-        in_specs=[
-            pl.BlockSpec((1, 8, chunk), lambda i: (i, 0, 0)),
-            pl.BlockSpec(values.shape, lambda i: (0, 0)),
-            pl.BlockSpec(tiles.shape, lambda i: (0, 0, 0)),
+        functools.partial(gather_kernel, views, reps),
+        out_shape=(
+            jax.ShapeDtypeStruct((views, *own.shape), f32),
+            jax.ShapeDtypeStruct(rows.shape, f32),
+        ),
+        in_specs=[vmem] * 5,
+        out_specs=(vmem, vmem),
+        scratch_shapes=[
+            pltpu.VMEM((tile, chunk), f32),
+            pltpu.VMEM(measured.shape, f32),
+            pltpu.VMEM((views * reps, *measured.shape), f32),
+            dma((views,)),
+            dma((views,)),
+            dma((views * reps,)),
+            dma((views * reps,)),
         ],
-        out_specs=pl.BlockSpec((rows, tile), lambda i: (0, 0)),
-        scratch_shapes=[pltpu.VMEM((tile, chunk), f32)],
-        compiler_params=pltpu.CompilerParams(vmem_limit_bytes=32 * 1024 * 1024),
+        compiler_params=pltpu.CompilerParams(
+            collective_id=0, has_side_effects=True, vmem_limit_bytes=48 * 1024 * 1024
+        ),
         cost_estimate=pl.CostEstimate(
-            flops=2 * chunks * chunk * tiles.size, bytes_accessed=2 * tiles.size, transcendentals=0
+            flops=4 * info.shape[0] * chunk * tiles.size,
+            bytes_accessed=8 * own.size * views,
+            transcendentals=0,
         ),
-    )(info, values, tiles)
+    )(info, rows, tiles, measured, own)
+
+
+def split_product(left, right):
+    return (
+        contract(left[0], right[0], 1, 0)
+        + contract(left[1], right[0], 1, 0)
+        + contract(left[0], right[1], 1, 0)
+    )
+
+
+def coil_kernel(
+    views,
+    reps,
+    gathered_ref,
+    maps_ref,
+    kspace_ref,
+    acquired_ref,
+    column_high,
+    column_low,
+    row_high,
+    row_low,
+    out_ref,
+    buffers,
+    total,
+    resid,
+    grads,
+    arrived,
+    send_rep,
+    recv_rep,
+    send_view,
+    recv_view,
+):
+    view, rep = lax.axis_index("view"), lax.axis_index("rep")
+    rows, width = maps_ref.shape[1], maps_ref.shape[2]
+    row_block = gathered_ref.shape[2]
+    halves = 2
+    part = rows // halves
+    near = [{"view": view, "rep": lax.rem(rep + step, reps)} for step in range(1, reps)]
+    far = [{"view": lax.rem(view + step, views), "rep": rep} for step in range(1, views)]
+    greet(near + far)
+    sends = []
+
+    def columns(stage, half, real, imag, sign):
+        table = (column_high[...], column_low[...])
+        out = split_product(split_data(jnp.concatenate([real, imag], axis=0)), table)
+        where = pl.ds(half * part, part)
+        buffers[stage, 0, where, :width] = out[:part, :width] + sign * out[part:, width:]
+        buffers[stage, 0, where, width:] = out[part:, :width] - sign * out[:part, width:]
+        for step in range(1, reps):
+            index = (stage * halves + half) * reps + step
+            copy = remote(
+                buffers.at[stage, 0, where],
+                buffers.at[stage, step, where],
+                send_rep.at[index],
+                recv_rep.at[index],
+                near[step - 1],
+            )
+            copy.start()
+            sends.append(copy)
+
+    def row_products(stage):
+        for step in range(reps):
+            if step:
+                for half in range(halves):
+                    sends[(stage * halves + half) * (reps - 1) + step - 1].wait_recv()
+            where = pl.ds(step * rows, rows)
+            table = (row_high[:, where], row_low[:, where])
+            product = split_product(table, split_data(buffers[stage, step]))
+            if step:
+                total[...] += product
+            else:
+                total[...] = product
+
+    blocks = part // row_block
+    for half in range(halves):
+        where = pl.ds(half * part, part)
+        real = gathered_ref[half * blocks : (half + 1) * blocks, 0].reshape(part, width)
+        imag = gathered_ref[half * blocks : (half + 1) * blocks, 1].reshape(part, width)
+        map_re, map_im = maps_ref[0, where], maps_ref[1, where]
+        columns(0, half, map_re * real - map_im * imag, map_re * imag + map_im * real, 1.0)
+    row_products(0)
+    acquired = acquired_ref[...]
+    resid[0] = acquired * (total[:rows, :width] + total[rows:, width:] - kspace_ref[0])
+    resid[1] = acquired * (total[:rows, width:] - total[rows:, :width] - kspace_ref[1])
+    for half in range(halves):
+        where = pl.ds(half * part, part)
+        columns(1, half, resid[0, where], resid[1, where], -1.0)
+    row_products(1)
+    image_re = total[:rows, :width] - total[rows:, width:]
+    image_im = total[:rows, width:] + total[rows:, :width]
+    map_re, map_im = maps_ref[0], maps_ref[1]
+    grads[:, 0] = (map_re * image_re + map_im * image_im).reshape(views, row_block, width)
+    grads[:, 1] = (map_re * image_im - map_im * image_re).reshape(views, row_block, width)
+    copies = []
+    for step in range(1, views):
+        device = far[step - 1]
+        copy = remote(
+            grads.at[device["view"]],
+            arrived.at[step],
+            send_view.at[step],
+            recv_view.at[step],
+            device,
+        )
+        copy.start()
+        copies.append(copy)
+    out_ref[...] = grads[view]
+    for step in range(1, views):
+        copies[step - 1].wait_recv()
+        out_ref[...] += arrived[step]
+    for copy in copies + sends:
+        copy.wait_send()
+
+
+def coil_call(views, reps, gathered, maps, kspace, acquired, tables):
+    rows, width = maps.shape[1:]
+    vmem = pl.BlockSpec(memory_space=pltpu.VMEM)
+    dma = pltpu.SemaphoreType.DMA
+    return pl.pallas_call(
+        functools.partial(coil_kernel, views, reps),
+        out_shape=jax.ShapeDtypeStruct(gathered.shape[1:], f32),
+        in_specs=[vmem] * 8,
+        out_specs=vmem,
+        scratch_shapes=[
+            pltpu.VMEM((2, reps, rows, 2 * width), f32),
+            pltpu.VMEM((2 * rows, 2 * width), f32),
+            pltpu.VMEM((2, rows, width), f32),
+            pltpu.VMEM(gathered.shape, f32),
+            pltpu.VMEM(gathered.shape, f32),
+            dma((4 * reps,)),
+            dma((4 * reps,)),
+            dma((views,)),
+            dma((views,)),
+        ],
+        compiler_params=pltpu.CompilerParams(
+            collective_id=1, has_side_effects=True, vmem_limit_bytes=48 * 1024 * 1024
+        ),
+        cost_estimate=pl.CostEstimate(
+            flops=96 * rows * width * width,
+            bytes_accessed=8 * gathered.size,
+            transcendentals=0,
+        ),
+    )(gathered, maps, kspace, acquired, *tables)
 
 
 def on_device(
@@ -148,7 +381,8 @@
     sampling,
 ):
     rep_count = lax.axis_size("rep")
-    owner_count = lax.axis_size("view") * rep_count
+    view_count = lax.axis_size("view")
+    owner_count = view_count * rep_count
     slab_count = lax.axis_size("slab")
     rep_at = lax.axis_index("rep")
     slab_at = lax.axis_index("slab")
@@ -166,9 +400,6 @@
     chain = [(i, i + 1) for i in range(slab_count - 1)]
     slice_after = lax.ppermute(own_images, "slab", [(b, a) for a, b in chain])
 
-    gathered = lax.all_gather(images[1:3, 0], "view", axis=1, tiled=True)
-    own_image = gathered.reshape(2, groups * row_block, width)
-
     own_blocks = row_block * width // tile_size
     local = pixel_blocks - owner_at * own_blocks
     live = jnp.arange(capacity, dtype=jnp.int32)[None] < counts[:, None]
@@ -179,72 +410,36 @@
     info = jnp.concatenate(lists + [jnp.zeros_like(lists[0])] * 5, axis=1)
     pixel_rows = own_images[0].astype(bf16).reshape(-1, tile_size)
     bin_rows = sinogram.shape[1] // tile_size
-    projected = tile_call(project_kernel, info, pixel_rows, proj_tiles, bin_rows)
-    full_sino = lax.psum(projected, ("view", "rep"))
-    measured = sinogram[0].reshape(bin_rows, tile_size).astype(f32)
-    pet_residual = (full_sino - measured).astype(bf16)
-    pet_term = tile_call(back_kernel, info, pet_residual, proj_tiles, own_blocks)
+    measured = sinogram[0].reshape(bin_rows, tile_size)
+    gathered, pet_term = gather_call(
+        view_count, rep_count, info, pixel_rows, proj_tiles, measured, own_images[1:3]
+    )
     pet_term = pet_term.reshape(row_block, width)
 
     grid = np.arange(width)
     angle = (np.outer(grid, grid) % width) * (2.0 * np.pi / width)
     cosine, sine = np.cos(angle) / np.sqrt(width), np.sin(angle) / np.sqrt(width)
     by_rep = grid.reshape(groups, rep_count, row_block).transpose(1, 0, 2).reshape(rep_count, -1)
-    rep_major = by_rep.reshape(-1)
-    row_tables = np.stack(
-        [
-            np.concatenate([table[rows][:, rep_major] for table in (cosine, sine)], axis=0)
-            for rows in by_rep
-        ]
-    )
-    row_high, row_low = (
-        lax.dynamic_index_in_dim(jnp.asarray(part), rep_at, keepdims=False)
-        for part in split_table(row_tables)
-    )
-    forward = np.block([[cosine, -sine], [sine, cosine]])
-    inverse = np.block([[cosine, sine], [-sine, cosine]])
-
-    def columns(real, imag, table):
-        high, low = split_data(jnp.concatenate([real, imag], axis=1))
-        table_high, table_low = (jnp.asarray(part) for part in split_table(table))
-        return (
-            contract(high, table_high, 1, 0)
-            + contract(low, table_high, 1, 0)
-            + contract(high, table_low, 1, 0)
+    row_tables = []
+    for rep in range(rep_count):
+        seen = np.concatenate([by_rep[(rep - step) % rep_count] for step in range(rep_count)])
+        row_tables.append(
+            np.concatenate([table[by_rep[rep]][:, seen] for table in (cosine, sine)], axis=0)
         )
-
-    def rows(values):
-        both = lax.all_gather(values, "rep", axis=0, tiled=True)
-        high, low = split_data(both)
-        out = (
-            contract(row_high, high, 1, 0)
-            + contract(row_high, low, 1, 0)
-            + contract(row_low, high, 1, 0)
-        )
-        half = out.shape[0] // 2
-        return (
-            out[:half, :width],
-            out[:half, width:],
-            out[half:, :width],
-            out[half:, width:],
-        )
-
-    sens = coil_maps.reshape(2, groups * row_block, width)
-    coil_re = sens[0] * own_image[0] - sens[1] * own_image[1]
-    coil_im = sens[0] * own_image[1] + sens[1] * own_image[0]
-    cos_re, cos_im, sin_re, sin_im = rows(columns(coil_re, coil_im, forward))
-    measured_k = kspace.reshape(2, groups * row_block, width)
-    acquired = sampling.reshape(-1).astype(f32)[:, None]
-    resid_re = acquired * (cos_re + sin_im - measured_k[0])
-    resid_im = acquired * (cos_im - sin_re - measured_k[1])
-    cos_re, cos_im, sin_re, sin_im = rows(columns(resid_re, resid_im, inverse))
-    image_re = cos_re - sin_im
-    image_im = cos_im + sin_re
-    grad_re = sens[0] * image_re + sens[1] * image_im
-    grad_im = sens[0] * image_im - sens[1] * image_re
-    coil_rows = jnp.stack([grad_re, grad_im]).reshape(2, groups, row_block, width)
-    coil_gradient = lax.psum_scatter(coil_rows, "view", scatter_dimension=1, tiled=True)
-    data_gradient = jnp.concatenate([pet_term[None], coil_gradient[:, 0]], axis=0)
+    tables = [jnp.asarray(part) for part in split_table(np.concatenate([cosine, sine], axis=1))]
+    for part in split_table(np.stack(row_tables)):
+        tables.append(lax.dynamic_index_in_dim(jnp.asarray(part), rep_at, keepdims=False))
+    rows = groups * row_block
+    coil_gradient = coil_call(
+        view_count,
+        rep_count,
+        gathered,
+        coil_maps.reshape(2, rows, width),
+        kspace.reshape(2, rows, width),
+        sampling.reshape(rows, 1).astype(f32),
+        tables,
+    )
+    data_gradient = jnp.concatenate([pet_term[None], coil_gradient], axis=0)
 
     global_rows = owner_at * row_block + jnp.arange(row_block, dtype=jnp.int32)
     row_keep = (global_rows < width - 1).astype(f32)[None, :, None]

time: 157 us -> 107 us (0.68)
  the two profiles are of different devices: /device:TPU:0 before, /device:TPU:14 now
where the time goes in v2:
time: 107 us; the launch traced here: 106 us
  Pallas kernels  76.8 us (72%)
  starting transfers between devices  8.44 us (8%)
  waiting for transfers between devices  7.67 us (7%)
  local copies, waits for them, and re-layouts  7.11 us (7%)
  other arithmetic  5.39 us (5%)
    pallas_call x1, Pallas kernels, gather_call(): pl.pallas_call(functools.partial(gather_kernel, views, reps), out_shape=(...  39.4 us
    pallas_call x1, Pallas kernels, coil_call(): pl.pallas_call(functools.partial(coil_kernel, views, reps), out_shape=jax...  37.3 us
    ppermute x1, waiting for transfers between devices, on_device(): slice_before = lax.ppermute(couple_slices, 'slab', chain)  6.54 us
    ppermute x1, starting transfers between devices, on_device(): slice_after = lax.ppermute(own_images, 'slab', [(b, a) for a, b in chain])  3.32 us
    unnamed x3, other arithmetic  3.03 us
  transfers between devices with their start and end apart: 4, of which 2 were waited for; matrix products, arithmetic and copies ran while one was open for 8% of the time, Pallas kernels for 72%

profile of v2, /device:TPU:14, one launch (start us, length us, event | category | flops | bytes accessed | tf_op | source)
XLA Modules:
  0.0 106.3 jit_solution(4113800645565938629)
XLA Ops:
  0.6 0.0 copy-start.4
  0.6 0.0 copy-start.10
  0.7 0.0 copy-start.7
  0.7 0.0 copy-start.11
  0.7 0.0 copy-start.8
  0.7 0.0 copy-start.9
  0.7 3.3 %collective-permute-start.1 = (f32[3,64,512]{2,1,0:T(8,128)}, f32[3,64,512]{2,1,0:T(8,128)}, u32[]{:S(2)}, u32[]{:S(2)}) collective-permute-start(f32[3,64,512]{2,1,0:T(8,128)} %bitcast.72), channel_id=1, source_target_pairs={{2,0},{3,1},{6,4},{7,5},{10,8},{11,9},{14,12},{15,13},{18,16},{19,... | collective-permute-start | bytes 1179656 | tf_op jit(solution)/shard_map/ppermute | solution.py:401
  4.0 0.8 slice.61
  4.8 1.9 %collective-permute-start = (f32[3,1,512]{2,1,0:T(1,128)S(1)}, f32[3,1,512]{2,1,0:T(1,128)S(1)}, u32[]{:S(2)}, u32[]{:S(2)}) collective-permute-start(f32[3,1,512]{2,1,0:T(1,128)S(1)} %slice.61), channel_id=1, source_target_pairs={{1,0},{4,1},{5,4},{8,5},{9,8},{12,9},{13,12},{3,2},{6,3},{7,6},{10... | collective-permute-start | bytes 18440 | tf_op jit(solution)/shard_map/ppermute | solution.py:399
  6.7 0.9 slice.85
  7.7 0.9 slice_bitcast_fusion.5
  8.6 0.0 copy-start.6
  8.6 1.2 %slice_bitcast_fusion.2 = f32[3,1,64,511]{3,2,0,1:T(8,128)S(1)} fusion(f32[3,64,512]{2,1,0:T(8,128)} %bitcast.75), kind=kLoop, calls=%fused_computation.17 | loop fusion | bytes 784896 | tf_op jit(solution)/shard_map/concatenate | solution.py:449
  9.7 0.0 copy-done.4
  9.8 0.1 pad.16.clone
  9.9 0.0 copy-done.10
  9.9 0.0 copy-done.7
  9.9 0.1 broadcast_add_fusion
  10.0 0.0 copy-done.11
  10.0 0.0 copy-done.8
  10.0 0.1 fusion.17
  10.1 0.0 copy-done.9
  10.1 0.1 convert_element_type.29.rows_ref
  10.2 0.1 convert_element_type.35.acquired_ref
  10.4 0.0 copy-start
  10.4 0.0 copy-done.6
  10.4 0.1 reduce.2
  10.5 1.4 %dynamic-slice_bitcast_fusion = (bf16[512,512]{1,0:T(8,128)(2,1)S(1)}, bf16[512,512]{1,0:T(8,128)(2,1)S(1)}) fusion(bf16[2,512,512]{2,1,0:T(8,128)(2,1)} %constant.58.clone, s32[]{:T(128)S(6)} %select_n.10, bf16[2,512,512]{2,1,0:T(8,128)(2,1)} %constant.57.clone), kind=kLoop, calls=%fused_computation.9 | loop fusion | bytes 2097156 | tf_op jit(solution)/shard_map/jit(dynamic_index_in_dim)/squeeze | solution.py:431
  11.8 0.1 add_add_fusion.info_ref
  11.9 0.2 copy-done
  12.1 0.0 copy-start.1
  12.1 0.0 copy-start.2
  12.1 0.0 copy-start.3
  12.1 39.4 %shard_map.166 = (f32[4,2,64,512]{3,2,1,0:T(8,128)S(1)}, f32[256,128]{1,0:T(8,128)S(1)}) custom-call(s32[1,8,1024]{2,1,0:T(8,128)S(1)} %add_add_fusion.info_ref, bf16[256,128]{1,0:T(8,128)(2,1)S(1)} %convert_element_type.29.rows_ref, bf16[48,128,128]{2,1,0:T(8,128)(2,1)S(1)} %copy-done, bf16[64,128]{1,0:T(8,128)(2,1)S(1)} %bitcast.69, ...), custom_call_target="tpu_custom_call" | custom-call | flops 3221225472 | bytes 2097152 | tf_op jit(solution)/shard_map/pallas_call | solution.py:200
  51.5 0.0 copy-done.1
  51.5 0.0 copy-done.2
  51.5 0.0 copy-done.3
  51.5 37.3 %shard_map.167 = f32[2,64,512]{2,1,0:T(8,128)S(1)} custom-call(f32[4,2,64,512]{3,2,1,0:T(8,128)S(1)} %get-tuple-element.6.gathered_ref, f32[2,256,512]{2,1,0:T(8,128)S(1)} %bitcast.70, f32[2,256,512]{2,1,0:T(8,128)S(1)} %bitcast.71, f32[256,1]{1,0:T(8,128)S(1)} %convert_element_type.35.acquired_ref, bf16[512,1024]{1,0:T(8,128)(2,1)S(1)} %copy-done.3, ...), custom_call_target="tpu_custom_call" | custom-call | flops 6442450944 | bytes 2097152 | tf_op jit(solution)/shard_map/pallas_call | solution.py:343
  88.9 0.0 collective-permute-done
  89.0 0.2 fusion.8
  89.1 0.0 collective-permute-done.1
  89.1 1.1 multiply_bitcast_fusion.1
  90.2 0.1 pad_maximum_fusion
  90.3 0.0 copy-start.5
  90.3 0.1 copy.29
  90.4 1.2 %copy-done.5 = f32[9,1,64,512]{3,2,1,0:T(8,128)S(1)} copy-done((f32[9,1,64,512]{3,2,1,0:T(8,128)S(1)}, f32[9,1,64,512]{3,2,1,0:T(8,128)}, u32[]{:S(2)}) %copy-start.5) | copy-done | bytes 1179672
  91.6 0.3 multiply_reduce_fusion
  91.9 0.1 maximum_divide_fusion
  91.9 0.3 fusion
  92.3 1.3 %collective-permute-start.3 = (f32[3,64,512]{2,1,0:T(8,128)S(1)}, f32[3,64,512]{2,1,0:T(8,128)S(1)}, u32[]{:S(2)}, u32[]{:S(2)}) collective-permute-start(f32[3,64,512]{2,1,0:T(8,128)S(1)} %fusion.2), channel_id=1, source_target_pairs={{0,2},{1,3},{4,6},{5,7},{8,10},{9,11},{12,14},{13,15},{16,18},{17,... | collective-permute-start | bytes 1179656 | tf_op jit(solution)/shard_map/ppermute | solution.py:465
  93.6 0.1 fusion.4
  93.7 1.9 %collective-permute-start.2 = (f32[3,1,512]{2,1,0:T(1,128)S(1)}, f32[3,1,512]{2,1,0:T(1,128)S(1)}, u32[]{:S(2)}, u32[]{:S(2)}) collective-permute-start(f32[3,1,512]{2,1,0:T(1,128)S(1)} %slice.65), channel_id=1, source_target_pairs={{0,1},{1,4},{4,5},{5,8},{8,9},{9,12},{12,13},{2,3},{3,6},{6,7},{7,... | collective-permute-start | bytes 18440 | tf_op jit(solution)/shard_map/ppermute | solution.py:464
  95.6 1.8 %fusion.1 = (f32[9,1,64,512]{3,2,1,0:T(8,128)}, f32[9,1,64,512]{3,2,1,0:T(8,128)}) fusion(f32[64,512]{1,0:T(8,128)S(1)} %maximum_divide_fusion, f32[9,1,64,512]{3,2,1,0:T(8,128)S(1)} %copy-done.5, f32[3,3,64,512]{3,2,1,0:T(8,128)S(1)} %copy.29), kind=kLoop, calls=%fused_computation.5 | loop fusion | flops 884736 | bytes 4849664
  97.4 0.1 slice.68
  97.5 1.1 %collective-permute-done.2 = f32[3,1,512]{2,1,0:T(1,128)S(1)} collective-permute-done((f32[3,1,512]{2,1,0:T(1,128)S(1)}, f32[3,1,512]{2,1,0:T(1,128)S(1)}, u32[]{:S(2)}, u32[]{:S(2)}) %collective-permute-start.2) | collective-permute-done | bytes 6176 | tf_op jit(solution)/shard_map/ppermute | solution.py:464
  98.7 6.5 %collective-permute-done.3 = f32[3,64,512]{2,1,0:T(8,128)S(1)} collective-permute-done((f32[3,64,512]{2,1,0:T(8,128)S(1)}, f32[3,64,512]{2,1,0:T(8,128)S(1)}, u32[]{:S(2)}, u32[]{:S(2)}) %collective-permute-start.3) | collective-permute-done | bytes 393248 | tf_op jit(solution)/shard_map/ppermute | solution.py:465
  105.2 1.1 %fusion.7 = f32[3,1,64,512]{3,2,1,0:T(8,128)} fusion(f32[2,64,512]{2,1,0:T(8,128)S(1)} %shard_map.167, f32[1,64,512]{2,1,0:T(8,128)S(1)} %broadcast_in_dim_reshape.3, f32[3,64,512]{2,1,0:T(8,128)S(1)} %collective-permute-done.3, f32[3,64,512]{2,1,0:T(8,128)S(1)} %get-tuple-element.16, f32[3,64,512]{2,1,0:T(8,128)S(1)} %get-tuple-element.15, ...), kind=kLoop, calls=%fused_computation.22 | loop fusion | flops 1277952 | bytes 3538948
  (13 shorter events, 0.2 us)
Async XLA Ops:
  0.6 9.1 %copy-start.4 = (f32[3,1,64,512]{3,2,1,0:T(8,128)S(1)}, f32[3,1,64,512]{3,2,1,0:T(8,128)}, u32[]{:S(2)}) copy-start(f32[3,1,64,512]{3,2,1,0:T(8,128)} %param.15) | copy-start | bytes 1179652
  0.6 9.3 %copy-start.10 = (s32[1,4,1,64]{3,2,1,0:T(1,128)S(1)}, s32[1,4,1,64]{3,2,1,0:T(1,128)}, u32[]{:S(2)}) copy-start(s32[1,4,1,64]{3,2,1,0:T(1,128)} %param.25) | copy-start | bytes 3076
  0.7 9.3 %copy-start.7 = (s32[4,256]{1,0:T(4,128)S(1)}, s32[4,256]{1,0:T(4,128)}, u32[]{:S(2)}) copy-start(s32[4,256]{1,0:T(4,128)} %param.20) | copy-start | bytes 12292
  0.7 9.4 %copy-start.11 = (s32[4]{0:T(128)S(1)}, s32[4]{0:T(128)}, u32[]{:S(2)}) copy-start(s32[4]{0:T(128)} %param.21) | copy-start | bytes 52
  0.7 9.3 %copy-start.8 = (s32[4,256]{1,0:T(4,128)S(1)}, s32[4,256]{1,0:T(4,128)}, u32[]{:S(2)}) copy-start(s32[4,256]{1,0:T(4,128)} %param.19) | copy-start | bytes 12292
  0.7 9.4 %copy-start.9 = (s32[4,256]{1,0:T(4,128)S(1)}, s32[4,256]{1,0:T(4,128)}, u32[]{:S(2)}) copy-start(s32[4,256]{1,0:T(4,128)} %param.18) | copy-start | bytes 12292
  0.7 88.4 %collective-permute-start.1 = (f32[3,64,512]{2,1,0:T(8,128)}, f32[3,64,512]{2,1,0:T(8,128)}, u32[]{:S(2)}, u32[]{:S(2)}) collective-permute-start(f32[3,64,512]{2,1,0:T(8,128)} %bitcast.72), channel_id=1, source_target_pairs={{2,0},{3,1},{6,4},{7,5},{10,8},{11,9},{14,12},{15,13},{18,16},{19,... | collective-permute-start | bytes 1179656 | tf_op jit(solution)/shard_map/ppermute | solution.py:401
  4.8 84.1 %collective-permute-start = (f32[3,1,512]{2,1,0:T(1,128)S(1)}, f32[3,1,512]{2,1,0:T(1,128)S(1)}, u32[]{:S(2)}, u32[]{:S(2)}) collective-permute-start(f32[3,1,512]{2,1,0:T(1,128)S(1)} %slice.61), channel_id=1, source_target_pairs={{1,0},{4,1},{5,4},{8,5},{9,8},{12,9},{13,12},{3,2},{6,3},{7,6},{10... | collective-permute-start | bytes 18440 | tf_op jit(solution)/shard_map/ppermute | solution.py:399
  8.6 1.8 %copy-start.6 = (bf16[1,8192]{1,0:T(2,128)(2,1)S(1)}, bf16[1,8192]{1,0:T(2,128)(2,1)}, u32[]{:S(2)}) copy-start(bf16[1,8192]{1,0:T(2,128)(2,1)} %param.22) | copy-start | bytes 49156
  10.4 1.7 %copy-start = (bf16[48,128,128]{2,1,0:T(8,128)(2,1)S(1)}, bf16[48,128,128]{2,1,0:T(8,128)(2,1)}, u32[]{:S(2)}) copy-start(bf16[48,128,128]{2,1,0:T(8,128)(2,1)} %tiles_ref.1) | copy-start | bytes 4718596
  12.1 39.4 %copy-start.1 = (f32[2,1,1,4,1,64,512]{6,5,4,3,2,1,0:T(8,128)S(1)}, f32[2,1,1,4,1,64,512]{6,5,4,3,2,1,0:T(8,128)}, u32[]{:S(2)}) copy-start(f32[2,1,1,4,1,64,512]{6,5,4,3,2,1,0:T(8,128)} %param.23) | copy-start | bytes 3145732
  12.1 39.4 %copy-start.2 = (f32[2,1,1,4,1,64,512]{6,5,4,3,2,1,0:T(8,128)S(1)}, f32[2,1,1,4,1,64,512]{6,5,4,3,2,1,0:T(8,128)}, u32[]{:S(2)}) copy-start(f32[2,1,1,4,1,64,512]{6,5,4,3,2,1,0:T(8,128)} %param.24) | copy-start | bytes 3145732
  12.1 39.5 %copy-start.3 = (bf16[512,1024]{1,0:T(8,128)(2,1)S(1)}, bf16[512,1024]{1,0:T(8,128)(2,1)}, u32[]{:S(2)}) copy-start(bf16[512,1024]{1,0:T(8,128)(2,1)} %constant.55.clone.column_high) | copy-start | bytes 3145732
  90.3 1.3 %copy-start.5 = (f32[9,1,64,512]{3,2,1,0:T(8,128)S(1)}, f32[9,1,64,512]{3,2,1,0:T(8,128)}, u32[]{:S(2)}) copy-start(f32[9,1,64,512]{3,2,1,0:T(8,128)} %param.16) | copy-start | bytes 3538948
  92.3 12.9 %collective-permute-start.3 = (f32[3,64,512]{2,1,0:T(8,128)S(1)}, f32[3,64,512]{2,1,0:T(8,128)S(1)}, u32[]{:S(2)}, u32[]{:S(2)}) collective-permute-start(f32[3,64,512]{2,1,0:T(8,128)S(1)} %fusion.2), channel_id=1, source_target_pairs={{0,2},{1,3},{4,6},{5,7},{8,10},{9,11},{12,14},{13,15},{16,18},{17,... | collective-permute-start | bytes 1179656 | tf_op jit(solution)/shard_map/ppermute | solution.py:465
  93.7 4.9 %collective-permute-start.2 = (f32[3,1,512]{2,1,0:T(1,128)S(1)}, f32[3,1,512]{2,1,0:T(1,128)S(1)}, u32[]{:S(2)}, u32[]{:S(2)}) collective-permute-start(f32[3,1,512]{2,1,0:T(1,128)S(1)} %slice.65), channel_id=1, source_target_pairs={{0,1},{1,4},{4,5},{5,8},{8,9},{9,12},{12,13},{2,3},{3,6},{6,7},{7,... | collective-permute-start | bytes 18440 | tf_op jit(solution)/shard_map/ppermute | solution.py:464

commit v3 on v2

--- a/solution.py
+++ b/solution.py
@@ -124,107 +124,6 @@
     pl.semaphore_wait(barrier, len(devices))
 
 
-def gather_kernel(
-    views,
-    reps,
-    info_ref,
-    rows_ref,
-    tiles_ref,
-    measured_ref,
-    own_ref,
-    gathered_ref,
-    back_ref,
-    total,
-    sino,
-    slots,
-    send_rows,
-    recv_rows,
-    send_sino,
-    recv_sino,
-):
-    view, rep = lax.axis_index("view"), lax.axis_index("rep")
-    count = views * reps
-    me = view * reps + rep
-
-    def owner(index):
-        index = lax.rem(index, count)
-        return {"view": index // reps, "rep": lax.rem(index, reps)}
-
-    greet([owner(me + step) for step in range(1, count)])
-    copies = []
-    for step in range(1, views):
-        device = {"view": lax.rem(view + step, views), "rep": rep}
-        copy = remote(
-            own_ref, gathered_ref.at[view], send_rows.at[step], recv_rows.at[step], device
-        )
-        copy.start()
-        copies.append(copy)
-    gathered_ref[view] = own_ref[...]
-    sino[...] = jnp.zeros_like(sino)
-    for at in range(info_ref.shape[0]):
-        project(info_ref, at, rows_ref, tiles_ref, sino, total)
-    sums = []
-    for step in range(1, count):
-        copy = remote(
-            sino, slots.at[step], send_sino.at[step], recv_sino.at[step], owner(me + step)
-        )
-        copy.start()
-        sums.append(copy)
-    for copy in sums:
-        copy.wait()
-    full = sino[...]
-    for step in range(1, count):
-        full = full + slots[step]
-    resid = (full - measured_ref[...].astype(f32)).astype(bf16)
-    back_ref[...] = jnp.zeros_like(back_ref)
-    for at in range(info_ref.shape[0]):
-        back_project(info_ref, at, resid, tiles_ref, back_ref, total)
-    for step in range(1, views):
-        source = lax.rem(view + views - step, views)
-        remote(
-            own_ref,
-            gathered_ref.at[source],
-            send_rows.at[step],
-            recv_rows.at[step],
-            {"view": source, "rep": rep},
-        ).wait_recv()
-    for copy in copies:
-        copy.wait_send()
-
-
-def gather_call(views, reps, info, rows, tiles, measured, own):
-    chunk = info.shape[2]
-    tile = tiles.shape[1]
-    vmem = pl.BlockSpec(memory_space=pltpu.VMEM)
-    dma = pltpu.SemaphoreType.DMA
-    return pl.pallas_call(
-        functools.partial(gather_kernel, views, reps),
-        out_shape=(
-            jax.ShapeDtypeStruct((views, *own.shape), f32),
-            jax.ShapeDtypeStruct(rows.shape, f32),
-        ),
-        in_specs=[vmem] * 5,
-        out_specs=(vmem, vmem),
-        scratch_shapes=[
-            pltpu.VMEM((tile, chunk), f32),
-            pltpu.VMEM(measured.shape, f32),
-            pltpu.VMEM((views * reps, *measured.shape), f32),
-            dma((views,)),
-            dma((views,)),
-            dma((views * reps,)),
-            dma((views * reps,)),
-        ],
-        compiler_params=pltpu.CompilerParams(
-            collective_id=0, has_side_effects=True, vmem_limit_bytes=48 * 1024 * 1024
-        ),
-        cost_estimate=pl.CostEstimate(
-            flops=4 * info.shape[0] * chunk * tiles.size,
-            bytes_accessed=8 * own.size * views,
-            transcendentals=0,
-        ),
-    )(info, rows, tiles, measured, own)
-
-
 def split_product(left, right):
     return (
         contract(left[0], right[0], 1, 0)
@@ -233,36 +132,171 @@
     )
 
 
-def coil_kernel(
+def step_kernel(
     views,
     reps,
-    gathered_ref,
+    slabs,
+    info_ref,
+    rows_ref,
+    measured_ref,
+    images_ref,
+    acquired_ref,
+    tiles_hbm,
+    duals_hbm,
+    maps_hbm,
+    kspace_hbm,
+    column_high_hbm,
+    column_low_hbm,
+    row_high_hbm,
+    row_low_hbm,
+    updated_ref,
+    shrunk_ref,
+    dual_ref,
+    tiles_ref,
+    duals_ref,
     maps_ref,
     kspace_ref,
-    acquired_ref,
     column_high,
     column_low,
     row_high,
     row_low,
-    out_ref,
+    load_sems,
+    slots_total,
+    sino,
+    slots,
+    back,
+    gathered,
     buffers,
     total,
     resid,
     grads,
     arrived,
+    couple,
+    row_after,
+    slice_after,
+    row_before,
+    slice_before,
+    send_halo,
+    recv_halo,
+    send_rows,
+    recv_rows,
+    send_sino,
+    recv_sino,
     send_rep,
     recv_rep,
     send_view,
     recv_view,
 ):
-    view, rep = lax.axis_index("view"), lax.axis_index("rep")
+    view, rep, slab = lax.axis_index("view"), lax.axis_index("rep"), lax.axis_index("slab")
+    count = views * reps
+    me = view * reps + rep
     rows, width = maps_ref.shape[1], maps_ref.shape[2]
-    row_block = gathered_ref.shape[2]
+    row_block = images_ref.shape[1]
+
+    pairs = [
+        (tiles_hbm, tiles_ref),
+        (duals_hbm, duals_ref),
+        (maps_hbm, maps_ref),
+        (column_high_hbm, column_high),
+        (column_low_hbm, column_low),
+        (row_high_hbm.at[rep], row_high),
+        (row_low_hbm.at[rep], row_low),
+        (kspace_hbm, kspace_ref),
+    ]
+    loads = [
+        pltpu.make_async_copy(source, target, load_sems.at[at])
+        for at, (source, target) in enumerate(pairs)
+    ]
+    for load in loads:
+        load.start()
+
+    def owner(index):
+        index = lax.rem(index, count)
+        return {"view": index // reps, "rep": lax.rem(index, reps), "slab": slab}
+
+    def other_slab(step):
+        return {"view": view, "rep": rep, "slab": lax.rem(slab + step, slabs)}
+
+    near = [owner(view * reps + lax.rem(rep + step, reps)) for step in range(1, reps)]
+    far = [owner(lax.rem(view + step, views) * reps + rep) for step in range(1, views)]
+    side = [other_slab(step) for step in sorted({1, slabs - 1})]
+    greet([owner(me + step) for step in range(1, count)] + side)
+    halos = [
+        remote(
+            images_ref.at[:, 0:8], row_after, send_halo.at[0], recv_halo.at[0], owner(me + count - 1)
+        ),
+        remote(images_ref, slice_after, send_halo.at[1], recv_halo.at[1], other_slab(slabs - 1)),
+        remote(
+            couple.at[0, :, row_block - 8 : row_block],
+            row_before,
+            send_halo.at[2],
+            recv_halo.at[2],
+            owner(me + 1),
+        ),
+        remote(couple.at[2], slice_before, send_halo.at[3], recv_halo.at[3], other_slab(1)),
+    ]
+    halos[0].start()
+    halos[1].start()
+    own_mr = images_ref.at[1:3]
+    moves = []
+    for step in range(views - 1, 0, -1):
+        copy = remote(
+            own_mr, gathered.at[view], send_rows.at[step], recv_rows.at[step], far[step - 1]
+        )
+        copy.start()
+        moves.append(copy)
+    gathered[view] = images_ref[1:3]
+
+    sino[...] = jnp.zeros_like(sino)
+    loads[0].wait()
+    for at in range(info_ref.shape[0]):
+        project(info_ref, at, rows_ref, tiles_ref, sino, slots_total)
+    sums = []
+    for step in range(1, count):
+        copy = remote(
+            sino, slots.at[step], send_sino.at[step], recv_sino.at[step], owner(me + step)
+        )
+        copy.start()
+        sums.append(copy)
+
+    halos[0].wait_recv()
+    halos[1].wait_recv()
+    loads[1].wait()
+    shape = (row_block, width)
+    global_rows = lax.broadcasted_iota(jnp.int32, shape, 0) + me * row_block
+    row_keep = jnp.where(global_rows < width - 1, 1.0, 0.0)
+    column_keep = jnp.where(lax.broadcasted_iota(jnp.int32, shape, 1) < width - 1, 1.0, 0.0)
+    slice_keep = jnp.where(slab < slabs - 1, 1.0, 0.0)
+    keeps = (row_keep, column_keep, slice_keep)
+    squares = jnp.zeros(shape, f32)
+    for channel in range(3):
+        own = images_ref[channel]
+        nexts = (
+            jnp.concatenate([own[1:], row_after[channel, 0:1]], axis=0),
+            pltpu.roll(own, width - 1, 1),
+            slice_after[channel],
+        )
+        for way in range(3):
+            difference = (nexts[way] - own) * keeps[way]
+            spread = difference + duals_ref[3 * channel + way]
+            couple[way, channel] = difference
+            dual_ref[3 * channel + way] = spread
+            squares += spread * spread
+    magnitude = jnp.sqrt(squares)
+    factor = jnp.maximum(magnitude - kappa, 0.0) / jnp.maximum(magnitude, kappa)
+    for channel in range(3):
+        for way in range(3):
+            spread = dual_ref[3 * channel + way]
+            shrunk = spread * factor
+            dual = spread - shrunk
+            shrunk_ref[3 * channel + way] = shrunk
+            dual_ref[3 * channel + way] = dual
+            couple[way, channel] = (couple[way, channel] - shrunk + dual) * keeps[way]
+    halos[2].start()
+    halos[3].start()
+
     halves = 2
     part = rows // halves
-    near = [{"view": view, "rep": lax.rem(rep + step, reps)} for step in range(1, reps)]
-    far = [{"view": lax.rem(view + step, views), "rep": rep} for step in range(1, views)]
-    greet(near + far)
     sends = []
 
     def columns(stage, half, real, imag, sign):
@@ -296,11 +330,22 @@
             else:
                 total[...] = product
 
+    for load in loads[2:]:
+        load.wait()
+    for step in range(1, views):
+        source = lax.rem(view + views - step, views)
+        remote(
+            own_mr,
+            gathered.at[source],
+            send_rows.at[step],
+            recv_rows.at[step],
+            owner(source * reps + rep),
+        ).wait_recv()
     blocks = part // row_block
     for half in range(halves):
         where = pl.ds(half * part, part)
-        real = gathered_ref[half * blocks : (half + 1) * blocks, 0].reshape(part, width)
-        imag = gathered_ref[half * blocks : (half + 1) * blocks, 1].reshape(part, width)
+        real = gathered[half * blocks : (half + 1) * blocks, 0].reshape(part, width)
+        imag = gathered[half * blocks : (half + 1) * blocks, 1].reshape(part, width)
         map_re, map_im = maps_ref[0, where], maps_ref[1, where]
         columns(0, half, map_re * real - map_im * imag, map_re * imag + map_im * real, 1.0)
     row_products(0)
@@ -328,43 +373,99 @@
         )
         copy.start()
         copies.append(copy)
-    out_ref[...] = grads[view]
+
+    for copy in sums:
+        copy.wait()
+    full = sino[...]
+    for step in range(1, count):
+        full = full + slots[step]
+    pet_residual = (full - measured_ref[...].astype(f32)).astype(bf16)
+    back[...] = jnp.zeros_like(back)
+    for at in range(info_ref.shape[0]):
+        back_project(info_ref, at, pet_residual, tiles_ref, back, slots_total)
+
+    halos[2].wait_recv()
+    halos[3].wait_recv()
+    per_row = width // back.shape[1]
+    for channel in range(3):
+        across = couple[0, channel]
+        along = couple[1, channel]
+        adjoint = (
+            jnp.concatenate([row_before[channel, 7:8], across[:-1]], axis=0)
+            - across
+            + pltpu.roll(along, 1, 1)
+            - along
+            + slice_before[channel]
+            - couple[2, channel]
+        )
+        if channel:
+            gradient = grads[view, channel - 1]
+        else:
+            gradient = back[...].reshape(row_block, per_row, back.shape[1]).reshape(shape)
+        updated_ref[channel] = images_ref[channel] - step_size * (gradient + penalty * adjoint)
     for step in range(1, views):
         copies[step - 1].wait_recv()
-        out_ref[...] += arrived[step]
-    for copy in copies + sends:
+        updated_ref[1:3] += -step_size * arrived[step]
+    for copy in moves + copies + sends + halos:
         copy.wait_send()
 
 
-def coil_call(views, reps, gathered, maps, kspace, acquired, tables):
+def step_call(mesh_sizes, staged, loaded):
+    views, reps, slabs = mesh_sizes
+    info, rows_in, measured, images, acquired = staged
+    tiles, duals, maps, kspace = loaded[:4]
+    chunk = info.shape[2]
+    tile = tiles.shape[1]
     rows, width = maps.shape[1:]
+    count = views * reps
     vmem = pl.BlockSpec(memory_space=pltpu.VMEM)
     dma = pltpu.SemaphoreType.DMA
+    held = [pltpu.VMEM(value.shape, value.dtype) for value in loaded[:6]]
+    held += [pltpu.VMEM(value.shape[1:], value.dtype) for value in loaded[6:]]
+    pieces = (views, 2, *images.shape[1:])
+    edge = (3, 8, width)
     return pl.pallas_call(
-        functools.partial(coil_kernel, views, reps),
-        out_shape=jax.ShapeDtypeStruct(gathered.shape[1:], f32),
-        in_specs=[vmem] * 8,
-        out_specs=vmem,
-        scratch_shapes=[
+        functools.partial(step_kernel, views, reps, slabs),
+        out_shape=(
+            jax.ShapeDtypeStruct(images.shape, f32),
+            jax.ShapeDtypeStruct(duals.shape, f32),
+            jax.ShapeDtypeStruct(duals.shape, f32),
+        ),
+        in_specs=[vmem] * len(staged) + [pl.BlockSpec(memory_space=pl.ANY)] * len(loaded),
+        out_specs=(vmem, vmem, vmem),
+        scratch_shapes=held
+        + [
+            dma((len(loaded),)),
+            pltpu.VMEM((tile, chunk), f32),
+            pltpu.VMEM(measured.shape, f32),
+            pltpu.VMEM((count, *measured.shape), f32),
+            pltpu.VMEM(rows_in.shape, f32),
+            pltpu.VMEM(pieces, f32),
             pltpu.VMEM((2, reps, rows, 2 * width), f32),
             pltpu.VMEM((2 * rows, 2 * width), f32),
             pltpu.VMEM((2, rows, width), f32),
-            pltpu.VMEM(gathered.shape, f32),
-            pltpu.VMEM(gathered.shape, f32),
+            pltpu.VMEM(pieces, f32),
+            pltpu.VMEM(pieces, f32),
+            pltpu.VMEM((3, *images.shape), f32),
+            pltpu.VMEM(edge, f32),
+            pltpu.VMEM(images.shape, f32),
+            pltpu.VMEM(edge, f32),
+            pltpu.VMEM(images.shape, f32),
+            dma((4,)),
+            dma((4,)),
+            dma((views,)),
+            dma((views,)),
+            dma((count,)),
+            dma((count,)),
             dma((4 * reps,)),
             dma((4 * reps,)),
             dma((views,)),
             dma((views,)),
         ],
         compiler_params=pltpu.CompilerParams(
-            collective_id=1, has_side_effects=True, vmem_limit_bytes=48 * 1024 * 1024
+            collective_id=0, has_side_effects=True, vmem_limit_bytes=60 * 1024 * 1024
         ),
-        cost_estimate=pl.CostEstimate(
-            flops=96 * rows * width * width,
-            bytes_accessed=8 * gathered.size,
-            transcendentals=0,
-        ),
-    )(gathered, maps, kspace, acquired, *tables)
+    )(*staged, *loaded)
 
 
 def on_device(
@@ -384,9 +485,7 @@
     view_count = lax.axis_size("view")
     owner_count = view_count * rep_count
     slab_count = lax.axis_size("slab")
-    rep_at = lax.axis_index("rep")
-    slab_at = lax.axis_index("slab")
-    owner_at = lax.axis_index("view") * rep_count + rep_at
+    owner_at = lax.axis_index("view") * rep_count + lax.axis_index("rep")
     row_block = images.shape[2]
     width = images.shape[3]
     tile_size = proj_tiles.shape[1]
@@ -395,10 +494,6 @@
     groups = coil_maps.shape[3]
 
     own_images = images[:, 0]
-    ring = [(i, i + 1) for i in range(owner_count - 1)]
-    row_after = lax.ppermute(own_images[:, :1], ("view", "rep"), [(b, a) for a, b in ring])
-    chain = [(i, i + 1) for i in range(slab_count - 1)]
-    slice_after = lax.ppermute(own_images, "slab", [(b, a) for a, b in chain])
 
     own_blocks = row_block * width // tile_size
     local = pixel_blocks - owner_at * own_blocks
@@ -411,11 +506,6 @@
     pixel_rows = own_images[0].astype(bf16).reshape(-1, tile_size)
     bin_rows = sinogram.shape[1] // tile_size
     measured = sinogram[0].reshape(bin_rows, tile_size)
-    gathered, pet_term = gather_call(
-        view_count, rep_count, info, pixel_rows, proj_tiles, measured, own_images[1:3]
-    )
-    pet_term = pet_term.reshape(row_block, width)
-
     grid = np.arange(width)
     angle = (np.outer(grid, grid) % width) * (2.0 * np.pi / width)
     cosine, sine = np.cos(angle) / np.sqrt(width), np.sin(angle) / np.sqrt(width)
@@ -427,51 +517,19 @@
             np.concatenate([table[by_rep[rep]][:, seen] for table in (cosine, sine)], axis=0)
         )
     tables = [jnp.asarray(part) for part in split_table(np.concatenate([cosine, sine], axis=1))]
-    for part in split_table(np.stack(row_tables)):
-        tables.append(lax.dynamic_index_in_dim(jnp.asarray(part), rep_at, keepdims=False))
+    tables += [jnp.asarray(part) for part in split_table(np.stack(row_tables))]
     rows = groups * row_block
-    coil_gradient = coil_call(
-        view_count,
-        rep_count,
-        gathered,
-        coil_maps.reshape(2, rows, width),
-        kspace.reshape(2, rows, width),
-        sampling.reshape(rows, 1).astype(f32),
-        tables,
-    )
-    data_gradient = jnp.concatenate([pet_term[None], coil_gradient], axis=0)
-
-    global_rows = owner_at * row_block + jnp.arange(row_block, dtype=jnp.int32)
-    row_keep = (global_rows < width - 1).astype(f32)[None, :, None]
-    slice_keep = (slab_at < slab_count - 1).astype(f32)
-    column_keep = (jnp.arange(width) < width - 1).astype(f32)[None, None, :]
-    next_row = jnp.concatenate([own_images[:, 1:], row_after], axis=1)
-    next_column = jnp.concatenate([own_images[..., 1:], own_images[..., :1]], axis=-1)
-    diff_rows = (next_row - own_images) * row_keep
-    diff_columns = (next_column - own_images) * column_keep
-    diff_slices = (slice_after - own_images) * slice_keep
-    differences = jnp.stack([diff_rows, diff_columns, diff_slices], axis=1).reshape(
-        9, row_block, width
-    )
-    spread = differences + scaled_duals[:, 0]
-    magnitude = jnp.sqrt(jnp.sum(spread * spread, axis=0))
-    shrunk = spread * (jnp.maximum(magnitude - kappa, 0.0) / jnp.maximum(magnitude, kappa))[None]
-    dual_next = spread - shrunk
-    coupling = (differences - shrunk + dual_next).reshape(3, 3, row_block, width)
-    couple_rows = coupling[:, 0] * row_keep
-    couple_columns = coupling[:, 1] * column_keep
-    couple_slices = coupling[:, 2] * slice_keep
-    row_before = lax.ppermute(couple_rows[:, -1:], ("view", "rep"), ring)
-    slice_before = lax.ppermute(couple_slices, "slab", chain)
-    adjoint = (
-        jnp.concatenate([row_before, couple_rows[:, :-1]], axis=1)
-        - couple_rows
-        + jnp.concatenate([couple_columns[..., -1:], couple_columns[..., :-1]], axis=-1)
-        - couple_columns
-        + slice_before
-        - couple_slices
-    )
-    updated = own_images - step_size * (data_gradient + penalty * adjoint)
+    updated, shrunk, dual_next = step_call(
+        (view_count, rep_count, slab_count),
+        (info, pixel_rows, measured, own_images, sampling.reshape(rows, 1).astype(f32)),
+        (
+            proj_tiles,
+            scaled_duals[:, 0],
+            coil_maps.reshape(2, rows, width),
+            kspace.reshape(2, rows, width),
+            *tables,
+        ),
+    )
     return (updated[:, None], shrunk[:, None], dual_next[:, None])
 
 

time: 107 us -> 82.5 us (0.77)
  the two profiles are of different devices: /device:TPU:14 before, /device:TPU:0 now
where the time goes in v3:
time: 82.5 us; the launch traced here: 82.1 us
  Pallas kernels  68.6 us (83%)
  local copies, waits for them, and re-layouts  8.45 us (10%)
  other arithmetic  4.35 us (5%)
    pallas_call x1, Pallas kernels, step_call(): pl.pallas_call(functools.partial(step_kernel, views, reps, slabs), out_sh...  68.6 us
    unnamed x5, local copies, waits for them, and re-layouts  5.24 us

profile of v3, /device:TPU:0, one launch (start us, length us, event | category | flops | bytes accessed | tf_op | source)
XLA Modules:
  0.0 82.1 jit_solution(5634739669242426907)
XLA Ops:
  0.6 0.1 pad.3.clone
  0.7 0.7 convert_reduce_fusion
  1.4 0.8 broadcast_add_fusion
  2.2 0.8 fusion.2
  3.0 0.7 reshape.47
  3.7 1.4 %reduce = bf16[8192]{0:T(1024)(128)(2,1)} reduce(bf16[1,8192]{1,0:T(2,128)(2,1)} %param.22, bf16[]{:T(256)} %constant.39), dimensions={0}, to_apply=%param.22.reduce_sub_computation | reduce | bytes 32770 | tf_op args[7]
  5.1 0.7 add_add_fusion.info_ref
  5.8 0.9 %slice.8 = bf16[1,1,64,512]{3,2,1,0:T(8,128)(2,1)S(1)} slice(f32[3,1,64,512]{3,2,1,0:T(8,128)} %param.15), slice={[0:1], [0:1], [0:64], [0:512]} | slice | bytes 131072 | tf_op jit(solution)/shard_map/slice | solution.py:506
  6.7 0.7 convert_element_type.10.rows_ref
  7.4 0.8 convert_element_type.13.acquired_ref
  8.2 68.6 %shard_map.166 = (f32[3,64,512]{2,1,0:T(8,128)}, f32[9,64,512]{2,1,0:T(8,128)}, f32[9,64,512]{2,1,0:T(8,128)}) custom-call(s32[1,8,1024]{2,1,0:T(8,128)} %add_add_fusion.info_ref, bf16[256,128]{1,0:T(8,128)(2,1)} %convert_element_type.10.rows_ref, bf16[64,128]{1,0:T(8,128)(2,1)} %bitcast.23, f32[3,64,512]{2,1,0:T(8,128)} %bitcast.21, ...), custom_call_target="tpu_custom_call" | custom-call | tf_op jit(solution)/shard_map/pallas_call | solution.py:427
  76.8 1.8 %copy.28 = f32[3,1,64,512]{3,2,1,0:T(8,128)} copy(f32[3,1,64,512]{3,2,1,0:T(8,128)} %bitcast.22) | data formatting | bytes 786432
  78.6 0.0 copy-start
  78.6 2.5 %copy.29 = f32[9,1,64,512]{3,2,1,0:T(8,128)} copy(f32[9,1,64,512]{3,2,1,0:T(8,128)} %bitcast.18) | data formatting | bytes 2359296
  81.1 0.0 copy-done
  81.1 1.0 %copy.30 = f32[9,1,64,512]{3,2,1,0:T(8,128)} copy(f32[9,1,64,512]{3,2,1,0:T(8,128)S(1)} %bitcast.17) | data formatting | bytes 2359296
  (4 shorter events, 0.0 us)
Async XLA Ops:
  78.6 2.5 %copy-start = (f32[9,64,512]{2,1,0:T(8,128)S(1)}, f32[9,64,512]{2,1,0:T(8,128)}, u32[]{:S(2)}) copy-start(f32[9,64,512]{2,1,0:T(8,128)} %get-tuple-element.8) | copy-start | bytes 3538948

commit v4 on v3

--- a/solution.py
+++ b/solution.py
@@ -136,11 +136,13 @@
     views,
     reps,
     slabs,
-    info_ref,
-    rows_ref,
-    measured_ref,
+    counts_ref,
+    ids_ref,
+    blocks_ref,
+    offsets_ref,
+    sinogram_ref,
     images_ref,
-    acquired_ref,
+    sampling_ref,
     tiles_hbm,
     duals_hbm,
     maps_hbm,
@@ -161,6 +163,10 @@
     row_high,
     row_low,
     load_sems,
+    info_ref,
+    rows_ref,
+    measured_ref,
+    acquired_ref,
     slots_total,
     sino,
     slots,
@@ -247,6 +253,27 @@
         moves.append(copy)
     gathered[view] = images_ref[1:3]
 
+    sectors, capacity = ids_ref.shape
+    per_chunk = sectors // info_ref.shape[0]
+    tile = tiles_ref.shape[1]
+    own_blocks = rows_ref.shape[0]
+    sector_bins = sinogram_ref.shape[1] // sectors
+    for sector in range(sectors):
+        at, lanes = sector // per_chunk, pl.ds(sector % per_chunk * capacity, capacity)
+        pick = slice(sector, sector + 1)
+        local = blocks_ref[pick] - me * own_blocks
+        slot = lax.broadcasted_iota(jnp.int32, (1, capacity), 1)
+        live = (slot < counts_ref[sector]) & (local >= 0) & (local < own_blocks)
+        info_ref[at, 0:1, lanes] = jnp.where(live, local, -1)
+        info_ref[at, 1:2, lanes] = ids_ref[pick]
+        info_ref[at, 2:3, lanes] = offsets_ref[pick] + sector * sector_bins
+    rows_ref[...] = (
+        images_ref[0]
+        .reshape(row_block, width // tile, tile)
+        .reshape(own_blocks, tile)
+        .astype(bf16)
+    )
+
     sino[...] = jnp.zeros_like(sino)
     loads[0].wait()
     for at in range(info_ref.shape[0]):
@@ -258,6 +285,19 @@
         )
         copy.start()
         sums.append(copy)
+
+    measured = sinogram_ref[...].astype(f32)
+    for row in range(measured_ref.shape[0]):
+        measured_ref[row : row + 1] = measured[:, row * tile : (row + 1) * tile]
+    square = (row_block, row_block)
+    diagonal = lax.broadcasted_iota(jnp.int32, square, 0) == lax.broadcasted_iota(
+        jnp.int32, square, 1
+    )
+    for group in range(rows // row_block):
+        flags = sampling_ref[group : group + 1].astype(f32)
+        acquired_ref[group * row_block : (group + 1) * row_block] = jnp.sum(
+            jnp.where(diagonal, flags, 0.0), axis=1, keepdims=True
+        )
 
     halos[0].wait_recv()
     halos[1].wait_recv()
@@ -379,7 +419,7 @@
     full = sino[...]
     for step in range(1, count):
         full = full + slots[step]
-    pet_residual = (full - measured_ref[...].astype(f32)).astype(bf16)
+    pet_residual = (full - measured_ref[...]).astype(bf16)
     back[...] = jnp.zeros_like(back)
     for at in range(info_ref.shape[0]):
         back_project(info_ref, at, pet_residual, tiles_ref, back, slots_total)
@@ -412,12 +452,16 @@
 
 def step_call(mesh_sizes, staged, loaded):
     views, reps, slabs = mesh_sizes
-    info, rows_in, measured, images, acquired = staged
+    counts, ids, _, _, sinogram, images, _ = staged
     tiles, duals, maps, kspace = loaded[:4]
-    chunk = info.shape[2]
+    sectors, capacity = ids.shape
+    per_chunk = min(4, sectors)
+    chunk = per_chunk * capacity
     tile = tiles.shape[1]
     rows, width = maps.shape[1:]
     count = views * reps
+    own_shape = (images.shape[1] * width // tile, tile)
+    bins_shape = (sinogram.shape[1] // tile, tile)
     vmem = pl.BlockSpec(memory_space=pltpu.VMEM)
     dma = pltpu.SemaphoreType.DMA
     held = [pltpu.VMEM(value.shape, value.dtype) for value in loaded[:6]]
@@ -431,15 +475,21 @@
             jax.ShapeDtypeStruct(duals.shape, f32),
             jax.ShapeDtypeStruct(duals.shape, f32),
         ),
-        in_specs=[vmem] * len(staged) + [pl.BlockSpec(memory_space=pl.ANY)] * len(loaded),
+        in_specs=[pl.BlockSpec(memory_space=pltpu.SMEM)]
+        + [vmem] * (len(staged) - 1)
+        + [pl.BlockSpec(memory_space=pl.ANY)] * len(loaded),
         out_specs=(vmem, vmem, vmem),
         scratch_shapes=held
         + [
             dma((len(loaded),)),
+            pltpu.VMEM((sectors // per_chunk, 8, chunk), jnp.int32),
+            pltpu.VMEM(own_shape, bf16),
+            pltpu.VMEM(bins_shape, f32),
+            pltpu.VMEM((rows, 1), f32),
             pltpu.VMEM((tile, chunk), f32),
-            pltpu.VMEM(measured.shape, f32),
-            pltpu.VMEM((count, *measured.shape), f32),
-            pltpu.VMEM(rows_in.shape, f32),
+            pltpu.VMEM(bins_shape, f32),
+            pltpu.VMEM((count, *bins_shape), f32),
+            pltpu.VMEM(own_shape, f32),
             pltpu.VMEM(pieces, f32),
             pltpu.VMEM((2, reps, rows, 2 * width), f32),
             pltpu.VMEM((2 * rows, 2 * width), f32),
@@ -483,29 +533,13 @@
 ):
     rep_count = lax.axis_size("rep")
     view_count = lax.axis_size("view")
-    owner_count = view_count * rep_count
     slab_count = lax.axis_size("slab")
-    owner_at = lax.axis_index("view") * rep_count + lax.axis_index("rep")
     row_block = images.shape[2]
     width = images.shape[3]
-    tile_size = proj_tiles.shape[1]
-    sectors, capacity = tile_ids.shape
-    sector_bins = sinogram.shape[1] // sectors
     groups = coil_maps.shape[3]
 
     own_images = images[:, 0]
 
-    own_blocks = row_block * width // tile_size
-    local = pixel_blocks - owner_at * own_blocks
-    live = jnp.arange(capacity, dtype=jnp.int32)[None] < counts[:, None]
-    local = jnp.where(live & (local >= 0) & (local < own_blocks), local, -1)
-    start = tof_offsets + sector_bins * jnp.arange(sectors, dtype=jnp.int32)[:, None]
-    chunk = 4 * capacity
-    lists = [part.reshape(-1, 1, chunk) for part in (local, tile_ids, start)]
-    info = jnp.concatenate(lists + [jnp.zeros_like(lists[0])] * 5, axis=1)
-    pixel_rows = own_images[0].astype(bf16).reshape(-1, tile_size)
-    bin_rows = sinogram.shape[1] // tile_size
-    measured = sinogram[0].reshape(bin_rows, tile_size)
     grid = np.arange(width)
     angle = (np.outer(grid, grid) % width) * (2.0 * np.pi / width)
     cosine, sine = np.cos(angle) / np.sqrt(width), np.sin(angle) / np.sqrt(width)
@@ -521,7 +555,15 @@
     rows = groups * row_block
     updated, shrunk, dual_next = step_call(
         (view_count, rep_count, slab_count),
-        (info, pixel_rows, measured, own_images, sampling.reshape(rows, 1).astype(f32)),
+        (
+            counts,
+            tile_ids,
+            pixel_blocks,
+            tof_offsets,
+            sinogram,
+            own_images,
+            sampling.reshape(groups, row_block),
+        ),
         (
             proj_tiles,
             scaled_duals[:, 0],

time: 82.5 us -> 74.9 us (0.908)
  other arithmetic: 4.35 us -> 0 us
  local copies, waits for them, and re-layouts: 8.45 us -> 5.24 us
    convert_element_type x2 -> x0, local copies, waits for them, and re-layouts: 1.47 us -> none  [the longest x1 0.79 us: on_device(): sampling.reshape(rows, 1).astype(f32)]
    unnamed x1 -> x0, other arithmetic: 1.45 us -> none
    slice x1 -> x0, local copies, waits for them, and re-layouts: 0.91 us -> none  [on_device(): pixel_rows = own_images[0].astype(bf16).reshape(-1, tile_size)]
where the time goes in v4:
time: 74.9 us; the launch traced here: 74.6 us
  Pallas kernels  68.8 us (92%)
  local copies, waits for them, and re-layouts  5.24 us (7%)
    pallas_call x1, Pallas kernels, step_call(): pl.pallas_call(functools.partial(step_kernel, views, reps, slabs), out_sh...  68.8 us
    unnamed x5, local copies, waits for them, and re-layouts  5.24 us

profile of v4, /device:TPU:0, one launch (start us, length us, event | category | flops | bytes accessed | tf_op | source)
XLA Modules:
  0.0 74.6 jit_solution(13250255376231362564)
XLA Ops:
  0.6 68.8 %shard_map.166 = (f32[3,64,512]{2,1,0:T(8,128)}, f32[9,64,512]{2,1,0:T(8,128)}, f32[9,64,512]{2,1,0:T(8,128)}) custom-call(s32[4]{0:T(128)} %counts_ref.1, s32[4,256]{1,0:T(4,128)} %ids_ref.1, s32[4,256]{1,0:T(4,128)} %blocks_ref.1, s32[4,256]{1,0:T(4,128)} %offsets_ref.1, bf16[1,8192]{1,0:T(2,128)(2,1)} %sinogram_ref.1, f32[3,64,512]{2,1,0:T(8,128)} %bitcast.19, ...), custom_call_target="tpu_custom_call" | custom-call | tf_op jit(solution)/shard_map/pallas_call | solution.py:471
  69.4 1.8 %copy.24 = f32[3,1,64,512]{3,2,1,0:T(8,128)} copy(f32[3,1,64,512]{3,2,1,0:T(8,128)} %bitcast.20) | data formatting | bytes 786432
  71.2 0.0 copy-start
  71.2 2.5 %copy.25 = f32[9,1,64,512]{3,2,1,0:T(8,128)} copy(f32[9,1,64,512]{3,2,1,0:T(8,128)} %bitcast.15) | data formatting | bytes 2359296
  73.6 0.0 copy-done
  73.6 1.0 %copy.26 = f32[9,1,64,512]{3,2,1,0:T(8,128)} copy(f32[9,1,64,512]{3,2,1,0:T(8,128)S(1)} %bitcast.14) | data formatting | bytes 2359296
Async XLA Ops:
  71.2 2.5 %copy-start = (f32[9,64,512]{2,1,0:T(8,128)S(1)}, f32[9,64,512]{2,1,0:T(8,128)}, u32[]{:S(2)}) copy-start(f32[9,64,512]{2,1,0:T(8,128)} %get-tuple-element.8) | copy-start | bytes 3538948
